TPU v7x, 32 devices: a whole 2x2x4 slice. The times are simulated.
32 devices in a mesh: level: 2 (over x), row: 8 (over z, core), col: 2 (over y).
Axes of the slice: x: 2, y: 2, z: 4, core: 2. Of those that a mesh axis runs over, the one named last changes fastest.
Arguments:
- noise: bfloat16 [64, 512, 512], P('row', ('level', 'col')), may hold values from -6 to 6
- source: bfloat16 [64, 512, 512], P('row', ('level', 'col')), may hold values from -16 to 16
Outputs:
- fine_pressure: float32 [64, 512, 512], P('row', ('level', 'col'))
- coarse_pressure: float32 [32, 256, 256], P('row', ('level', 'col'))
All inputs are finite; a program needn't handle non-finite values.
Results may differ from a plain program's by a relative error of at most 0.00035.
Values sent between devices are 32-bit elements; how exact they have to be, the bound alone decides.
No kernel may reach another device: no remote copies, remote signals or barrier semaphores. Data moves between devices by JAX's collectives and lax.ppermute only.
A program may use at most 256 MiB of HBM per device.

v0:
```python
import functools
import math

import jax
import jax.numpy as jnp
import numpy as np
from jax import lax
from jax.experimental import pallas as pl
from jax.experimental.pallas import tpu as pltpu
from jax.sharding import PartitionSpec as P

JACOBI_WEIGHT = 2.0 / 3.0
CORRELATION = 0.2
FIELD_SCALE = 0.3
DECAY = (2.0 * math.pi * CORRELATION) ** 2
EVERY = ("row", "level", "col")
PLANE = ("level", "col")
MIB = 1 << 20
SUB, LANE = 8, 128
HALO = 4


def two_parts(matrix):
    high = matrix.astype(jnp.bfloat16)
    low = (matrix - high.astype(np.float64)).astype(jnp.bfloat16)
    return high, low


def angles(rows, cols, length):
    return 2.0 * np.pi * (np.outer(rows, cols) % length) / length


def third_modes(devices, js):
    return np.array([[d + devices * j for j in js] for d in range(devices)])


def forward_third(length, devices, js):
    theta = angles(third_modes(devices, js).reshape(-1), np.arange(length), length)
    return np.stack([np.cos(theta), -np.sin(theta)], axis=1).reshape(-1, length)


def inverse_third(length, devices, js):
    modes = third_modes(devices, js).reshape(devices // 2, 2, len(js)).transpose(1, 0, 2)
    theta = 2.0 * np.pi * (modes[..., None] * np.arange(length // 2) % length) / length
    both = np.stack([np.cos(theta), -np.sin(theta)], axis=3)
    return both.reshape(2, -1, length // 2)


def second_modes(length):
    return np.arange(length // 2).reshape(-1, 2).T


def second_table(length):
    theta = second_modes(length)[:, None, :] * np.arange(length // 2)[None, :, None]
    theta = 2.0 * np.pi * (theta % length) / length
    return np.concatenate([np.cos(theta), np.sin(theta)], axis=2)


def forward_first(length):
    theta = angles(np.arange(length), np.arange(length), length)
    cos, sin = np.cos(theta), np.sin(theta)
    return np.block([[cos, sin], [-sin, cos]])


def inverse_first(length):
    theta = angles(np.arange(length), np.arange(length), length)
    cos, sin = np.cos(theta), np.sin(theta)
    cos[:, length // 2] = 0.0
    sin[:, length // 2] = 0.0
    return np.block([[cos, -sin], [sin, cos]])


def inverse_first_coarse(length, rows):
    full = inverse_first(length)
    value = full.reshape(2, rows, length // rows, 2 * length)
    turned = np.concatenate([-full[length:], full[:length]]).reshape(value.shape)
    order = lambda x: x.transpose(1, 0, 2, 3).reshape(2 * length, 2 * length)
    return np.concatenate([order(value), order(turned)])


def second_coarse(length, groups):
    theta = angles(second_modes(length).reshape(-1), np.arange(length), length)
    table = np.concatenate([np.cos(theta), np.sin(theta)])
    span = length // groups
    out = np.zeros((2, length, groups, 2, span))
    for pair in range(2):
        out[pair, :, :, pair, :] = table.reshape(length, groups, span)
    return out.reshape(2 * length, 2 * length)


def third_coarse(length, devices, js):
    modes = third_modes(devices, js).reshape(devices, len(js) // 2, 2)
    theta = 2.0 * np.pi * (modes[..., None] * np.arange(length) % length) / length
    both = np.stack([np.cos(theta), -np.sin(theta)])
    return both.transpose(0, 2, 1, 3, 4).reshape(2 * (len(js) // 2) * devices, 2 * length)


def third_coarse_halo(length, devices, js):
    theta = angles(third_modes(devices, js).reshape(-1), np.arange(length), length)
    return np.concatenate([np.cos(theta), -np.sin(theta)], axis=1)


def lane_order(parts, coarse_parts):
    out = np.zeros((LANE, LANE))
    for h in range(HALO):
        for q in range(parts):
            out[HALO * q + h, parts * h + q] = 1.0
        for j in range(coarse_parts):
            out[LANE // 2 + HALO * j + h, LANE // 2 + coarse_parts * h + j] = 1.0
    return out


def split(x):
    high = x.astype(jnp.bfloat16)
    return high, (x - high.astype(jnp.float32)).astype(jnp.bfloat16)


def dot(a, b):
    return lax.dot_general(a, b, (((1,), (0,)), ((), ())), preferred_element_type=jnp.float32)


def dot_t(a, b):
    return lax.dot_general(a, b, (((1,), (1,)), ((), ())), preferred_element_type=jnp.float32)


def stacked(matrix):
    high, low = two_parts(matrix)
    return np.block([[high, high], [low, np.zeros_like(low)]])


def dot_left(stack, x):
    value = dot(stack, jnp.concatenate(split(x), axis=0))
    rows = stack.shape[0] // 2
    return value[:rows] + value[rows:]


def dot3(a, b):
    (ah, al), (bh, bl) = a, b
    return dot(ah, bh) + (dot(ah, bl) + dot(al, bh))


def load(pairs, sems):
    copies = [pltpu.make_async_copy(a, b, sems.at[i]) for i, (a, b) in enumerate(pairs)]
    for copy in copies:
        copy.start()
    return copies


def send(pairs, sems, first):
    copies = [pltpu.make_async_copy(a, b, sems.at[first + i]) for i, (a, b) in enumerate(pairs)]
    for copy in copies:
        copy.start()
    return copies


def forward_kernel(planes, d_hbm, x_hbm, out_hbm, d, x, out, sems):
    pieces, rows = d.shape[0], d.shape[1] // 2
    parts = [slice(p * LANE, (p + 2) * LANE) for p in range(0, planes, 2)]
    pairs = [(x_hbm.at[at, :], x.at[at, :]) for at in parts]
    copies = load([(d_hbm.at[0], d.at[0])] + pairs + [(d_hbm.at[i], d.at[i]) for i in range(1, pieces)], sems)
    sent = []
    copies[0].wait()
    for piece in range(pieces):
        if piece:
            copies[len(parts) + piece].wait()
        for i, at in enumerate(parts):
            if piece == 0:
                copies[i + 1].wait()
            value = dot_t(d[piece], x[at, :])
            value = value[:rows] + value[rows:]
            for h in range(2):
                out[pl.ds(piece * rows * SUB + 2 * i + h, rows, stride=SUB), :] = value[
                    :, h * LANE : (h + 1) * LANE
                ]
        tall = slice(piece * rows * SUB, (piece + 1) * rows * SUB)
        sent += send([(out.at[tall, :], out_hbm.at[tall, :])], sems, len(copies) + piece)
    for copy in sent:
        copy.wait()


def middle_kernel(sizes, scale, b, *rest):
    (first, second, rows, groups, js, low) = sizes
    count = 9
    away, out_hbm, near, rest = (
        rest[:count],
        rest[count],
        rest[count + 1 : 2 * count + 1],
        rest[2 * count + 1 :],
    )
    out, sems, zh, zl, y, oh, ol, qh, ql = rest
    copies = load(list(zip(away, near)), sems)
    csh, csl, forward, inverse, coarse_inverse, cch, ccl, ch, cl = near
    q_count = 2 * js
    half, quarter = second // 2, second // 4
    for q in range(q_count):
        for g in range(groups // 2):
            for r in range(0, rows, 2):
                at = r * groups + g
                near_half = jnp.concatenate([b[at, q], b[at + groups, q]], axis=0)
                at += groups // 2
                far_half = jnp.concatenate([b[at, q], b[at + groups, q]], axis=0)
                at = slice(q * first + r * SUB, q * first + (r + 2) * SUB)
                lanes = slice(g * LANE, (g + 1) * LANE)
                zh[0, at, lanes], zl[0, at, lanes] = split(near_half + far_half)
                zh[1, at, lanes], zl[1, at, lanes] = split(near_half - far_half)
    for copy in copies[:5]:
        copy.wait()
    wide = 8 * first
    for top in range(0, q_count * first, wide):
        at = slice(top, top + wide)
        for parity in range(2):
            y[parity, at, :] = dot3(
                (zh[parity, at, :], zl[parity, at, :]), (csh[parity], csl[parity])
            )
    mode0 = lax.broadcasted_iota(jnp.int32, (first, second), 0)
    mode0 = jnp.where(mode0 < first // 2, mode0, mode0 - first).astype(jnp.float32)
    lane = lax.broadcasted_iota(jnp.int32, (first, second), 1)
    mode1 = jnp.where(lane < half, lane, lane - half)
    mode1 = jnp.where(mode1 < quarter, 2 * mode1, 2 * (mode1 - quarter) + 1).astype(jnp.float32)
    base = 1.0 + DECAY * (mode0 * mode0 + mode1 * mode1)
    for j in range(js):
        top = j * 2 * first
        re, im = slice(top, top + first), slice(top + first, top + 2 * first)
        cos, sin = slice(0, quarter), slice(quarter, half)
        whole = lambda part, lanes: jnp.concatenate(
            [y[0, part, lanes], y[1, part, lanes]], axis=1
        )
        rc, rs, ic, isn = whole(re, cos), whole(re, sin), whole(im, cos), whole(im, sin)
        wave = jnp.concatenate(
            [
                jnp.concatenate([rc + isn, rc - isn], axis=1),
                jnp.concatenate([ic - rs, ic + rs], axis=1),
            ],
            axis=0,
        )
        spectrum = dot_left(forward[...], wave)
        amp = jnp.where(lane == half, 0.0, scale[j, 1] / (base + scale[j, 0]))
        scaled = spectrum * jnp.concatenate([amp, amp], axis=0)
        field = dot_left(inverse[...], scaled)
        plus, minus = field[:, :half], field[:, half:]
        even, odd = plus + minus, plus - minus
        odd = jnp.concatenate([-odd[first:], odd[:first]], axis=0)
        at = slice(top, top + 2 * first)
        for parity, lanes in enumerate((cos, sin)):
            operand = jnp.concatenate([even[:, lanes], odd[:, lanes]], axis=1)
            oh[parity, at, :], ol[parity, at, :] = split(operand)
        if j < low:
            keep = first // 4
            kept = [
                scaled[at : at + keep, :]
                for at in (0, first - keep, first, 2 * first - keep)
            ]
            band = jnp.concatenate(kept, axis=0)
            low_lane = lax.broadcasted_iota(jnp.int32, (first, quarter), 1) < quarter // 2
            pieces = []
            for at in (0, half):
                upper = pltpu.roll(band[:, at + quarter : at + half], quarter // 2, 1)
                pieces.append(jnp.where(low_lane, band[:, at : at + quarter], upper))
            band = jnp.concatenate(pieces, axis=1)
            field = dot_left(coarse_inverse[...], band)
            value, turned = field[:first], field[first:]
            operand = jnp.concatenate(
                [
                    value[:, :quarter] + value[:, quarter:],
                    turned[:, :quarter] - turned[:, quarter:],
                ],
                axis=1,
            )
            at = slice(j // 2 * first, (j // 2 + 1) * first)
            lanes = slice(j % 2 * half, (j % 2 + 1) * half)
            qh[at, lanes], ql[at, lanes] = split(operand)
    for copy in copies[5:]:
        copy.wait()
    copies = []
    wide = 4 * first
    lane = lax.broadcasted_iota(jnp.int32, (SUB, LANE), 1)
    extra = q_count + low // 2

    def leave(start, stop):
        at = slice(start, stop)
        copies.extend(send([(out.at[:, at], out_hbm.at[:, at])], sems, len(copies)))

    def give(value, start):
        tiles = value.shape[0] // first
        for q in range(tiles):
            for r in range(rows):
                for g in range(groups):
                    at = q * first + r * SUB
                    out[r * groups + g, start + q] = value[
                        at : at + SUB, g * LANE : (g + 1) * LANE
                    ]
        leave(start, start + tiles)

    def halo_columns(value, start, held):
        tiles = value.shape[0] // first
        for r in range(rows):
            for g in range(groups):
                total = held[r, g]
                left = max(g - 1, 0) * LANE
                right = min(g + 1, groups - 1) * LANE
                for q in range(tiles):
                    at = slice(q * first + r * SUB, q * first + (r + 1) * SUB)
                    both = jnp.where(
                        lane < LANE // 2,
                        value[at, right : right + LANE],
                        value[at, left : left + LANE],
                    )
                    to = HALO * (start + q)
                    both = pltpu.roll(both, (to + 2) % LANE, 1)
                    total = jnp.where((lane >= to) & (lane < to + HALO), both, total)
                held[r, g] = total

    def coarse_columns(value, held):
        half_lane = LANE // 2
        for j in range(low):
            for r in range(rows):
                at = slice(j // 2 * first + r * SUB, j // 2 * first + (r + 1) * SUB)
                shift = HALO * j + 2 - j % 2 * half_lane
                to = half_lane + HALO * j
                for g in range(groups):
                    left = max(g - 1, 0) * LANE
                    right = min(g + 1, groups - 1) * LANE
                    left = pltpu.roll(value[at, left : left + LANE], shift % LANE, 1)
                    right = pltpu.roll(
                        value[at, right : right + LANE], (shift + half_lane) % LANE, 1
                    )
                    total = jnp.where((lane >= to) & (lane < to + 2), left, held[r, g])
                    held[r, g] = jnp.where(
                        (lane >= to + 2) & (lane < to + HALO), right, total
                    )

    columns = {
        (r, g): jnp.zeros((SUB, LANE), jnp.float32) for r in range(rows) for g in range(groups)
    }
    coarse = dot3((qh[...], ql[...]), (cch[...], ccl[...]))
    give(coarse, q_count)
    coarse_columns(coarse, columns)
    for top in range(0, q_count * first, wide):
        at = slice(top, top + wide)
        even, odd = (
            dot3((oh[parity, at, :], ol[parity, at, :]), (ch[parity], cl[parity]))
            for parity in range(2)
        )
        value = jnp.concatenate([even + odd, even - odd], axis=1)
        give(value, top // first)
        halo_columns(value, top // first, columns)
    for (r, g), total in columns.items():
        out[r * groups + g, extra] = total
    leave(extra, extra + 1)
    for copy in copies:
        copy.wait()


def gather_modes(b, at, sizes, lh, ll):
    devices, q_count, tiles = sizes
    for i, n in enumerate(at):
        for parity in range(2):
            rows = jnp.concatenate(
                [
                    b[pl.ds(s * tiles * SUB + n, q_count, stride=SUB), :]
                    for s in range(parity, devices, 2)
                ],
                axis=0,
            )
            to = slice(i * LANE, (i + 1) * LANE)
            lh[parity, to, :], ll[parity, to, :] = split(jnp.transpose(rows))


def inverse_pair(i, lh, ll, eh, el, ks, to, cells):
    at = slice(i * cells, (i + 2) * cells)
    even, odd = (
        dot3((lh[parity, at, :], ll[parity, at, :]), (eh[parity], el[parity]))
        for parity in range(2)
    )
    value = jnp.exp(jnp.concatenate([even + odd, even - odd], axis=1))
    for n in range(2):
        put_rows(ks, to + n, SUB, value[n * cells : (n + 1) * cells])


def edge_kernel(sizes, flags, b, *rest):
    (devices, q_count, low, tiles, planes, length) = sizes
    away, (ks, cks, cols, far, near_edge), rest = rest[:7], rest[7:12], rest[12:]
    near, (lh, ll, mh, ml, sems) = rest[:7], rest[7:]
    copies = load(list(zip(away, near)), sems)
    eh, el, ceh, cel, order, cwh, cwl = near
    cells, short = LANE, length // 2
    halves, coarse_planes = low // 2, planes // 2
    half = cells // 2
    gather_modes(b, (0, 1, planes - 2, planes - 1), (devices, q_count, tiles), lh, ll)
    for n in range(coarse_planes):
        rows = jnp.concatenate(
            [
                b[pl.ds((q_count + h) * SUB + c * coarse_planes + n, devices, stride=tiles * SUB), :]
                for c in range(2)
                for h in range(halves)
            ],
            axis=0,
        )
        at = slice(n * LANE, (n + 1) * LANE)
        mh[at, :], ml[at, :] = split(jnp.transpose(rows))

    for copy in copies[:4]:
        copy.wait()

    for i in range(0, 4, 2):
        inverse_pair(i, lh, ll, eh, el, ks, i, cells)
    value = dot3((mh[...], ml[...]), (ceh[...], cel[...]))
    for n in range(coarse_planes):
        top = n * cells
        part = value[top : top + half, :short] + value[top + half : top + cells, short:]
        part = jnp.exp(part)
        put_rows(cks, n, SUB, part)

    for copy in copies[4:]:
        copy.wait()
    lane = lax.broadcasted_iota(jnp.int32, (SUB, LANE), 1)
    tile_rows = [b[(s * tiles + tiles - 1) * SUB : (s + 1) * tiles * SUB, :] for s in range(devices)]
    high, rest_part = split(jnp.concatenate(tile_rows, axis=0))
    ordered = dot(high, order[...]) + dot(rest_part, order[...])

    def joined(of, width, start):
        fit = LANE // width
        cells_of = []
        for h in range(HALO):
            parts = []
            for i, s in enumerate(of):
                moved = ordered[s * SUB : (s + 1) * SUB]
                shift = (i % fit * width - start - h * width) % LANE
                moved = pltpu.roll(moved, shift, 1) if shift else moved
                if i % fit == 0:
                    parts.append(moved)
                else:
                    parts[-1] = jnp.where(lane >= i % fit * width, moved, parts[-1])
            cells_of.append(jnp.concatenate(parts, axis=1))
        return split(jnp.concatenate(cells_of, axis=0))

    even, odd = (
        dot3(joined(range(parity, devices, 2), q_count, 0), (eh[parity], el[parity]))
        for parity in range(2)
    )
    value = jnp.exp(jnp.concatenate([even + odd, even - odd], axis=1))
    cols[...] = value
    for h in range(HALO):
        for i, n in enumerate((0, 1, planes - 2, planes - 1)):
            at = h * planes + n
            put_rows(ks, i, halo_row(h, cells), value[at : at + 1, :])
    whole = dot3(joined(range(devices), low, LANE // 2), (cwh[...], cwl[...]))
    for h in range(HALO):
        top = h * SUB
        part = whole[top : top + coarse_planes, :short] + whole[top + coarse_planes : top + SUB, short:]
        part = jnp.exp(part)
        for n in range(coarse_planes):
            put_rows(cks, n, halo_row(h, half), part[n : n + 1, :])
    for held in (ks, cks):
        repeat_sides(flags, held, [(n,) for n in range(4)])
    odd_row = flags[4] == 1
    low_end = (jnp.where(odd_row, 2, 1), jnp.where(odd_row, 3, 0))
    high_end = (jnp.where(odd_row, 1, 2), jnp.where(odd_row, 0, 3))
    for edge, of in ((far, low_end), (near_edge, high_end)):
        at = 0
        for held in (ks, cks):
            count, end = held.shape[1], held.shape[2] - SUB
            for n in of:
                for x in range(count):
                    edge[at : at + end - SUB, :] = held[n, x, SUB:end, :]
                    at += end - SUB
            for x in range(count):
                edge[at + x : at + x + 1, :] = held[of[1], x, SUB - 1 : SUB, :]
                edge[at + count + x : at + count + x + 1, :] = held[of[1], x, end : end + 1, :]
            at += SUB


def halo_row(h, cells):
    return SUB - 2 + h if h < 2 else SUB + cells + h - 2


def source_kernel(planes, pairs, x, out, lo, hi, left, right, held, summed):
    cells = x.shape[0] // planes
    length = x.shape[1]
    half, fourth = cells // 2, cells // 4
    held[...] = dot(x[...], pairs[...])
    for n in range(planes // 2):
        top = 2 * n * cells
        for at in range(0, out.shape[1], LANE):
            lanes = slice(at, at + LANE)
            summed[...] = held[top : top + cells, lanes] + held[top + cells : top + 2 * cells, lanes]
            out[n * half : (n + 1) * half, lanes] = (
                summed[pl.ds(0, half, stride=2), :] + summed[pl.ds(1, half, stride=2), :]
            )
    for edge, plane in ((lo, 0), (hi, planes - 1)):
        edge[:cells, :] = x[plane * cells : (plane + 1) * cells, :].astype(jnp.float32)
        at = plane // 2 * half
        edge[cells:, : length // 2] = out[at : at + fourth, :]
        edge[cells:, length // 2 :] = out[at + fourth : at + half, :]
    for edge, row in ((left, 0), (right, cells - 1)):
        edge[...] = jnp.zeros_like(edge)
        for n in range(planes):
            at = n * cells + (row // SUB * SUB)
            edge[n : n + 1, :] = x[at : at + SUB, :].astype(jnp.float32)[row % SUB : row % SUB + 1]
        for n in range(planes // 2):
            at = n * half + row // 2
            edge[SUB + n : SUB + n + 1, : length // 2] = out[at : at + 1, :]


def beside(parts, ends):
    lane = lax.broadcasted_iota(jnp.int32, parts[0].shape, 1)
    ahead = [pltpu.roll(x, 1, 1) for x in parts]
    behind = [pltpu.roll(x, LANE - 1, 1) for x in parts]
    sums = []
    for i in range(len(parts)):
        left = jnp.where(lane == 0, ahead[i - 1] if i else ends[0], ahead[i])
        right = jnp.where(
            lane == LANE - 1, behind[i + 1] if i + 1 < len(parts) else ends[1], behind[i]
        )
        sums.append(left + right)
    return sums


def first_sweep(tiles, ext, mid, lower, upper, f, store):
    for top in range(0, ext, SUB):
        end = top + SUB
        parts = [mid(x, top, end) for x in range(tiles)]
        for x, both in enumerate(beside(parts, (parts[0], parts[-1]))):
            k = parts[x]
            above = pltpu.roll(k, 1, 0) if top == 0 else mid(x, top - 1, end - 1)
            below = pltpu.roll(k, SUB - 1, 0) if end == ext else mid(x, top + 1, end + 1)
            total = (lower(x, top, end) + upper(x, top, end)) + (above + below) + both
            scale = JACOBI_WEIGHT / (6.0 * k + total)
            u = f(x, top, end) * (2.0 * scale)
            store(x, top, end, u, k * u, scale)


def second_sweep(tiles, ext, k, u, w, r, store):
    for top in range(SUB, ext - SUB, SUB):
        end = top + SUB
        sums = []
        for lower, mid, upper in (u, w):
            parts = [mid(x, top, end) for x in range(tiles)]
            sums.append(
                [
                    both
                    + (lower(x, top, end) + upper(x, top, end))
                    + (mid(x, top - 1, end - 1) + mid(x, top + 1, end + 1))
                    for x, both in enumerate(beside(parts, (0.0, 0.0)))
                ]
            )
        for x in range(tiles):
            coupled = k(x, top, end) * sums[0][x] + sums[1][x]
            value = (2.0 - JACOBI_WEIGHT) * u[1](x, top, end) + r(x, top, end) * coupled
            store(x, top, end, value)


def plane_of(held, *at):
    return lambda x, top, end: held[(*at, x, slice(top, end), slice(None))]


def put_rows(held, to, at, rows):
    for x in range(held.shape[1]):
        held[to, x, at : at + rows.shape[0], :] = rows[:, x * LANE : (x + 1) * LANE]


def repeat_sides(flags, held, at):
    end = held.shape[-2] - SUB

    @pl.when(flags[2] == 1)
    def _():
        for p in at:
            held[(*p, slice(None), slice(SUB - 1, SUB))] = held[(*p, slice(None), slice(SUB, SUB + 1))]

    @pl.when(flags[3] == 1)
    def _():
        for p in at:
            held[(*p, slice(None), slice(end, end + 1))] = held[
                (*p, slice(None), slice(end - 1, end))
            ]


def put_block(fine, held, to, source, row, cells, length):
    if fine:
        put_rows(held, to, SUB, source[row : row + cells, :])
    else:
        half = cells // 2
        put_rows(held, to, SUB, source[row : row + half, :length])
        put_rows(held, to, SUB + half, source[row : row + half, length:])


def layout_kernel(sizes, *rest):
    away, outs, near, sems = rest[:6], rest[6:10], rest[10:16], rest[16]
    for copy in load(list(zip(away, near)), sems):
        copy.wait()
    source, coarse_source, *edges = near
    sides = edges[2:]
    for fine, inner, outer in ((True, *outs[:2]), (False, *outs[2:])):
        planes, cells, length = sizes if fine else [n // 2 for n in sizes]
        f = source if fine else coarse_source
        source_row = 0 if fine else SUB

        def plane(held, to, p):
            put_rows(held, to, SUB, f[p].astype(jnp.float32))
            for side, row in zip(sides, (SUB - 1, SUB + cells)):
                at = source_row + p
                put_rows(held, to, row, side[at : at + 1, :length])

        for p in range(1, planes - 1):
            plane(inner, p - 1, p)
        for group, p in enumerate((0, planes - 1)):
            row = 0 if fine else 2 * cells
            put_block(fine, outer.at[group], 0, edges[group], row, cells, length)
            plane(outer.at[group], 1, p)


def inner_level(sizes, ks, fs, us, ws, rs):
    planes, _, length = sizes
    tiles, ext = ks.shape[1:3]

    def first(p, carry):
        def store(x, top, end, u, w, r):
            at = (p - 1, x, slice(top, end))
            us[at], ws[at], rs[at] = u, w, r

        near = [plane_of(ks, p + i) for i in (0, -1, 1)]
        first_sweep(tiles, ext, *near, plane_of(fs, p - 1), store)
        return carry

    lax.fori_loop(1, planes - 1, first, 0)


def inner_kernel(sizes, shares, flags, b, eh_hbm, el_hbm, edges, cks, cols, fs, cfs, *rest):
    out_hbm, us, ws, rs, cus, cws, crs, ks, eh, el, lh, ll, out, sems = rest
    planes, cells, length = sizes
    tiles, ext = ks.shape[1:3]
    copies = load([(eh_hbm, eh), (el_hbm, el)], sems)
    middle = range(2, planes - 2)
    gather_modes(b, middle, shares, lh, ll)
    for i, p in enumerate((0, 1, planes - 2, planes - 1)):
        ks[p] = edges[i]
    for h in range(HALO):
        for p in middle:
            at = h * planes + p
            put_rows(ks, p, halo_row(h, cells), cols[at : at + 1, :])
    for copy in copies:
        copy.wait()
    for p in range(2, planes - 2, 2):
        inverse_pair(p - 2, lh, ll, eh, el, ks, p, cells)
    repeat_sides(flags, ks, [(p,) for p in middle])
    inner_level(sizes, ks, fs, us, ws, rs)

    def second(p, carry):
        def store(x, top, end, value):
            out[p - 2, top - SUB : end - SUB, x * LANE : (x + 1) * LANE] = value

        u, w = ([plane_of(held, p - 1 + i) for i in (-1, 0, 1)] for held in (us, ws))
        second_sweep(tiles, ext, plane_of(ks, p), u, w, plane_of(rs, p - 1), store)
        return carry

    lax.fori_loop(2, planes - 2, second, 0)
    copies = send([(out, out_hbm.at[2 : planes - 2])], sems, 0)
    inner_level([n // 2 for n in sizes], cks, cfs, cus, cws, crs)
    for copy in copies:
        copy.wait()


def outer_kernel(sizes, flags, *rest):
    kept, coarse_kept, (k_far, k_near, _, out, coarse_out), rest = (
        rest[:5],
        rest[5:10],
        rest[10:15],
        rest[15:],
    )
    scratch = (rest[:6], rest[6:])
    levels = (sizes, tuple(n // 2 for n in sizes))
    start = 0
    sent = []
    for size, held, given, target in zip(
        levels, scratch, (kept, coarse_kept), (out, coarse_out)
    ):
        planes = size[0]
        ks, fs, inner_us, inner_ws, inner_rs = given
        halo, us, ws, rs, done, sems = held
        tiles, ext = ks.shape[1:3]
        rows = size[1]
        for group, edge in ((flags[4], k_far), (1 - flags[4], k_near)):
            at = start
            for place in range(2 * tiles):
                to = place * ext + SUB
                halo[group, to : to + rows, :] = edge[at : at + rows, :]
                at += rows
            for x in range(tiles):
                to = (tiles + x) * ext
                halo[group, to + SUB - 1 : to + SUB, :] = edge[at + x : at + x + 1, :]
                to += SUB + rows
                halo[group, to : to + 1, :] = edge[at + tiles + x : at + tiles + x + 1, :]
        start = at + SUB
        for group in range(2):

            @pl.when(flags[group] == 1)
            def _():
                for x in range(tiles):
                    at = (tiles + x) * ext
                    halo[group, at : at + ext, :] = ks[3 * group, x]

        def both_ends(group, carry):
            def halo_plane(slot):
                def get(x, top, end):
                    at = (slot * tiles + x) * ext
                    return halo[group, at + top : at + end, :]

                return get

            inwards = lambda i, count: jnp.where(group == 0, i, count - 1 - i)
            own = [plane_of(ks, inwards(i, 4)) for i in range(2)]
            u, w = (
                [plane_of(new, group, i) for i in range(2)]
                + [plane_of(old, inwards(i, planes - 2)) for i in range(2)]
                for new, old in ((us, inner_us), (ws, inner_ws))
            )
            around = ((halo_plane(1), halo_plane(0), own[0]), (own[0], halo_plane(1), own[1]))
            for i, near in enumerate(around):

                def store(x, top, end, u, w, r):
                    at = (group, i, x, slice(top, end))
                    us[at], ws[at] = u, w
                    if i == 1:
                        rs[group, x, top:end, :] = r

                first_sweep(tiles, ext, *near, plane_of(fs, group, i), store)
            scales = (plane_of(rs, group), plane_of(inner_rs, inwards(0, planes - 2)))
            for i, r in enumerate(scales):

                def store(x, top, end, value):
                    done[group, i, top - SUB : end - SUB, x * LANE : (x + 1) * LANE] = value

                second_sweep(tiles, ext, own[i], u[i : i + 3], w[i : i + 3], r, store)
                pltpu.make_async_copy(
                    done.at[group, i], target.at[inwards(i, planes)], sems.at[2 * group + i]
                ).start()
            return carry

        lax.fori_loop(0, 2, both_ends, 0)
        for group, at in enumerate(((0, 1), (planes - 1, planes - 2))):
            for i, p in enumerate(at):
                sent.append(
                    pltpu.make_async_copy(
                        done.at[group, i], target.at[p], sems.at[2 * group + i]
                    )
                )
    for copy in sent:
        copy.wait()


SMEM = pl.BlockSpec(memory_space=pltpu.SMEM)
VMEM = pl.BlockSpec(memory_space=pltpu.VMEM)
AWAY = pl.BlockSpec(memory_space=pltpu.HBM)
ANY = pl.BlockSpec(memory_space=pl.ANY)


def call(kernel, outs, operands, scratch, flops, specs, limit, out_specs=None, aliases=None):
    many = isinstance(outs, (list, tuple))
    written = outs if many else [outs]
    moved = sum(math.prod(x.shape) * x.dtype.itemsize for x in (*operands, *written))
    operands = [
        pltpu.with_memory_space_constraint(x, pltpu.HBM) if spec is AWAY else x
        for x, spec in zip(operands, specs)
    ]
    out_specs = out_specs or [
        VMEM if isinstance(x, jax.ShapeDtypeStruct) else AWAY for x in written
    ]
    return pl.pallas_call(
        kernel,
        out_shape=outs,
        in_specs=specs,
        out_specs=out_specs if many else out_specs[0],
        scratch_shapes=scratch,
        input_output_aliases=aliases or {},
        compiler_params=pltpu.CompilerParams(vmem_limit_bytes=limit * MIB),
        cost_estimate=pl.CostEstimate(flops=flops, bytes_accessed=moved, transcendentals=0),
    )(*operands)


def f32(*shape):
    return jax.ShapeDtypeStruct(shape, jnp.float32)


def room(*arrays):
    return [pltpu.VMEM(x.shape, x.dtype) for x in arrays]


def chain(axis):
    up = [(i, i + 1) for i in range(lax.axis_size(axis) - 1)]
    return up, [(j, i) for i, j in up]


def swap(lo, hi, axis):
    up, down = chain(axis)
    return lax.ppermute(hi, axis, up), lax.ppermute(lo, axis, down)


def held_planes(size, *count):
    planes, cells, length = size
    return f32(*count, length // LANE, cells + 2 * SUB, LANE)


def outer_scratch(size):
    planes, cells, length = size
    return room(
        f32(2, 2 * (length // LANE) * (cells + 2 * SUB), LANE),
        held_planes(size, 2, 2),
        held_planes(size, 2, 2),
        held_planes(size, 2),
        f32(2, 2, cells, length),
    ) + [pltpu.SemaphoreType.DMA((4,))]


def fused_body(noise, source):
    rows, groups = lax.axis_size("row"), lax.axis_size(PLANE)
    devices = rows * groups
    planes, cells, length = noise.shape
    first, second = planes * rows, cells * groups
    bf16 = jnp.bfloat16
    held = length // 2 // devices
    js = list(range(held))
    low = held // 2
    me = lax.axis_index(EVERY)
    row_at, group_at = lax.axis_index("row"), lax.axis_index(PLANE)
    flags = jnp.stack(
        [
            row_at == 0,
            row_at == rows - 1,
            group_at == 0,
            group_at == groups - 1,
            row_at % 2 == 1,
        ]
    ).astype(jnp.int32)
    norm = FIELD_SCALE * (float(first) * float(second) * float(length)) ** (-0.5)
    flat = (planes * cells, length)

    pieces = 4
    table = [x.reshape(pieces, -1, length) for x in two_parts(forward_third(length, devices, js))]
    table = np.concatenate(table, axis=1)
    shape = (length * SUB, LANE)
    sent = call(
        functools.partial(forward_kernel, planes),
        pltpu.HBM(shape, jnp.float32),
        (table, noise.reshape(flat)),
        room(table)
        + [
            pltpu.VMEM(flat, bf16),
            pltpu.VMEM(shape, jnp.float32),
            pltpu.SemaphoreType.DMA((2 * pieces + planes // 2,)),
        ],
        4 * length * length * planes * cells,
        [AWAY] * 2,
        12,
    )
    sent, source = lax.optimization_barrier((sent, source))
    sent = sent.reshape(devices, 2 * held, SUB, LANE)
    arrived = lax.all_to_all(sent, EVERY, split_axis=0, concat_axis=0, tiled=True)

    pairs = np.zeros((length, length // 2), np.float32)
    pairs[np.arange(length), np.arange(length) // 2] = 0.125
    level = f32(cells + cells // 4, length)
    side = f32(2 * SUB, length)
    coarse_source, *edges = call(
        functools.partial(source_kernel, planes),
        [f32(planes * cells // 4, length // 2), level, level, side, side],
        (pairs.astype(bf16), source.reshape(flat)),
        [
            pltpu.VMEM((planes * cells, length // 2), jnp.float32),
            pltpu.VMEM((cells, LANE), jnp.float32),
        ],
        planes * cells * length * length,
        [VMEM] * 2,
        12,
    )
    coarse_source = coarse_source.reshape(planes // 2, cells // 2, length // 2)
    edges = (*swap(*edges[:2], "row"), *swap(*edges[2:], PLANE))
    arrived, edges, coarse_source = lax.optimization_barrier((arrived, edges, coarse_source))

    constants = (
        two_parts(second_table(second))
        + (
            stacked(forward_first(first)),
            stacked(inverse_first(first)),
            stacked(inverse_first_coarse(first // 2, rows)),
        )
        + two_parts(second_coarse(second // 2, groups))
        + two_parts(second_table(second).transpose(0, 2, 1))
    )
    tiles = 2 * held + low // 2 + 1
    modes = (me + devices * np.array(js)).astype(jnp.float32)
    weight = jnp.where(modes == 0.0, norm, 2.0 * norm).astype(jnp.float32)
    scale = jnp.stack([DECAY * modes * modes, weight], axis=1)
    block = (2, 2 * held * first, second // 2)
    shape = (devices, tiles, SUB, LANE)
    out = call(
        functools.partial(middle_kernel, (first, second, rows, groups, held, low)),
        pltpu.HBM(shape, jnp.float32),
        (scale, arrived, *constants),
        room(*constants)
        + [
            pltpu.VMEM(shape, jnp.float32),
            pltpu.SemaphoreType.DMA((len(constants),)),
            pltpu.VMEM(block, bf16),
            pltpu.VMEM(block, bf16),
            pltpu.VMEM(block, jnp.float32),
            pltpu.VMEM(block, bf16),
            pltpu.VMEM(block, bf16),
            pltpu.VMEM((low // 2 * first, second), bf16),
            pltpu.VMEM((low // 2 * first, second), bf16),
        ],
        6 * 2 * 2 * held * first * second * (second + 2 * first),
        [SMEM, VMEM] + [AWAY] * len(constants),
        22,
    )
    out, source, coarse_source, edges = lax.optimization_barrier(
        (out, source, coarse_source, edges)
    )
    got = lax.all_to_all(out, EVERY, split_axis=0, concat_axis=0, tiled=True)
    size, coarse_size = noise.shape, coarse_source.shape
    sizes = (size, coarse_size)
    sources = (source, coarse_source, *edges)
    laid = call(
        functools.partial(layout_kernel, size),
        [
            held_planes(s, *count)
            for s in sizes
            for count in ((s[0] - 2,), (2, 2))
        ],
        sources,
        room(*sources) + [pltpu.SemaphoreType.DMA((6,))],
        source.size,
        [AWAY] * 6,
        12,
    )
    got, laid = lax.optimization_barrier((got, laid))

    third = inverse_third(length, devices, js)
    constants = (
        two_parts(third)
        + two_parts(third_coarse(length // 2, devices, js[:low]))
        + (lane_order(2 * held, low).astype(bf16),)
        + two_parts(third_coarse_halo(length // 2, devices, js[:low]))
    )
    edge = f32(sum(2 * (s[2] // LANE) * s[1] + SUB for s in sizes), LANE)
    shares = (devices, 2 * held, tiles)
    got = got.reshape(devices * tiles * SUB, LANE)
    ks, coarse_ks, cols, far, near = call(
        functools.partial(edge_kernel, (devices, 2 * held, low, tiles, planes, length)),
        [held_planes(s, 4) for s in sizes] + [f32(HALO * planes, length), edge, edge],
        (flags, got, *constants),
        room(*constants)
        + [pltpu.VMEM((2, 4 * cells, devices * held), bf16)] * 2
        + [pltpu.VMEM((planes // 2 * LANE, devices * low), bf16)] * 2
        + [pltpu.SemaphoreType.DMA((7,))],
        3 * planes * cells * length * length,
        [SMEM, VMEM] + [AWAY] * 7,
        16,
    )
    k_far, k_near = (
        lax.ppermute(
            x, "row", [p for i in range(at, rows - 1, 2) for p in ((i, i + 1), (i + 1, i))]
        )
        for x, at in ((far, 1), (near, 0))
    )
    inner_f, outer_f, coarse_inner_f, coarse_outer_f = laid
    inner, *kept = call(
        functools.partial(inner_kernel, size, shares),
        [pltpu.HBM(size, jnp.float32)] + [held_planes(s, s[0] - 2) for s in sizes for _ in range(3)],
        (flags, got, *constants[:2], ks, coarse_ks, cols, inner_f, coarse_inner_f),
        room(held_planes(size, planes), *constants[:2])
        + [pltpu.VMEM((2, (planes - 4) * cells, devices * held), bf16)] * 2
        + room(f32(planes - 4, cells, length))
        + [pltpu.SemaphoreType.DMA((2,))],
        3 * planes * cells * length * length,
        [SMEM, VMEM] + [AWAY] * 2 + [VMEM] * 5,
        18,
    )
    return call(
        functools.partial(outer_kernel, size),
        [pltpu.HBM(s, jnp.float32) for s in sizes],
        (flags, ks, outer_f, *kept[:3], coarse_ks, coarse_outer_f, *kept[3:], k_far, k_near, inner),
        outer_scratch(size) + outer_scratch(coarse_size),
        30 * source.size,
        [SMEM] + [VMEM] * 12 + [AWAY],
        18,
        None,
        {13: 0},
    )


NEIGHBOUR_STEPS = ((1, 0, 0), (-1, 0, 0), (0, 1, 0), (0, -1, 0), (0, 0, 1), (0, 0, -1))


def padded(x, sides, width):
    for axis, dim in sides:
        peers, length = (lax.axis_size(axis), x.shape[dim])
        up = [(i, (i + 1) % peers) for i in range(peers - 1)]
        down = [(j, i) for i, j in up]
        last = lax.slice_in_dim(x, length - width, length, axis=dim)
        leading = lax.slice_in_dim(x, 0, width, axis=dim)
        before = lax.ppermute(last, axis, up)
        after = lax.ppermute(leading, axis, down)
        x = jnp.concatenate([before, x, after], axis=dim)
    return x


def signed_modes(index, length):
    return jnp.where(index < length // 2, index, index - length).astype(jnp.float32)


def amplitude(first_modes, second_modes, third_modes, first_edge, second_edge, third_edge):
    squared = first_modes * first_modes + second_modes * second_modes + third_modes * third_modes
    value = FIELD_SCALE / (1.0 + (2.0 * math.pi * CORRELATION) ** 2 * squared)
    edge = (
        (jnp.abs(first_modes) == first_edge)
        | (jnp.abs(second_modes) == second_edge)
        | (jnp.abs(third_modes) == third_edge)
    )
    return jnp.where(edge, 0.0, value)


def phase_table(count_rows, count_cols, modulus, sign):
    left_index = jnp.arange(count_rows, dtype=jnp.int32)[:, None]
    right_index = jnp.arange(count_cols, dtype=jnp.int32)[None, :]
    angle = 2.0 * math.pi / modulus * (left_index * right_index % modulus).astype(jnp.float32)
    return (jnp.cos(angle), sign * jnp.sin(angle))


def split_length(length):
    outer_len = 2 ** ((length.bit_length() - 1) // 2)
    return (outer_len, length // outer_len)


def real_form(form, left_value, right_value):
    return jnp.einsum(form, left_value, right_value, precision=lax.Precision.HIGHEST)


def complex_form(form, left_real, left_imag, right_real, right_imag):
    real_part = real_form(form, left_real, right_real) - real_form(form, left_imag, right_imag)
    imag_part = real_form(form, left_real, right_imag) + real_form(form, left_imag, right_real)
    return (real_part, imag_part)


def merge_pair(values, out_form, first_letter):
    merge_at = out_form.index(first_letter)
    out_dims = list(values.shape)
    merged = (
        out_dims[:merge_at]
        + [out_dims[merge_at] * out_dims[merge_at + 1]]
        + out_dims[merge_at + 2 :]
    )
    return values.reshape(merged)


def forward_axis(real_part, imag_part, lead_form, out_form, kept_modes):
    length = real_part.shape[-1]
    outer_len, inner_len = split_length(length)
    split_shape = real_part.shape[:-1] + (outer_len, inner_len)
    outer_real, outer_imag = phase_table(outer_len, outer_len, outer_len, -1.0)
    twist_real, twist_imag = phase_table(outer_len, inner_len, length, -1.0)
    inner_real, inner_imag = phase_table(inner_len, kept_modes // outer_len, inner_len, -1.0)
    first_form = lead_form + "ab,ai->" + lead_form + "ib"
    split_real = real_part.reshape(split_shape)
    if imag_part is None:
        section_real = real_form(first_form, split_real, outer_real)
        section_imag = real_form(first_form, split_real, outer_imag)
    else:
        section_real, section_imag = complex_form(
            first_form, split_real, imag_part.reshape(split_shape), outer_real, outer_imag
        )
    turned_real = section_real * twist_real - section_imag * twist_imag
    turned_imag = section_real * twist_imag + section_imag * twist_real
    result_real, result_imag = complex_form(
        lead_form + "ib,bj->" + out_form, turned_real, turned_imag, inner_real, inner_imag
    )
    return (merge_pair(result_real, out_form, "j"), merge_pair(result_imag, out_form, "j"))


def inverse_axis(real_part, imag_part, length, lead_form, out_form, real_only):
    kept_modes = real_part.shape[-1]
    outer_len, inner_len = split_length(length)
    split_shape = real_part.shape[:-1] + (kept_modes // outer_len, outer_len)
    inner_real, inner_imag = phase_table(kept_modes // outer_len, inner_len, inner_len, 1.0)
    twist_real, twist_imag = phase_table(outer_len, inner_len, length, 1.0)
    outer_real, outer_imag = phase_table(outer_len, outer_len, outer_len, 1.0)
    section_real, section_imag = complex_form(
        lead_form + "ji,jb->" + lead_form + "ib",
        real_part.reshape(split_shape),
        imag_part.reshape(split_shape),
        inner_real,
        inner_imag,
    )
    turned_real = section_real * twist_real - section_imag * twist_imag
    turned_imag = section_real * twist_imag + section_imag * twist_real
    second_form = lead_form + "ib,ia->" + out_form
    if real_only:
        result = real_form(second_form, turned_real, outer_real) - real_form(
            second_form, turned_imag, outer_imag
        )
        return merge_pair(result, out_form, "a")
    result_real, result_imag = complex_form(
        second_form, turned_real, turned_imag, outer_real, outer_imag
    )
    return (merge_pair(result_real, out_form, "a"), merge_pair(result_imag, out_form, "a"))


def low_band(values, half_coarse, fine_len):
    return jnp.concatenate(
        [values[:, :, :half_coarse], values[:, :, fine_len - half_coarse :]], axis=2
    )


def window(values, margin, offset):
    return values[
        margin + offset[0] : values.shape[0] - margin + offset[0],
        margin + offset[1] : values.shape[1] - margin + offset[1],
        margin + offset[2] : values.shape[2] - margin + offset[2],
    ]


def face_weight(center, beside):
    return jnp.where(beside > 0.0, 0.5 * (center + beside), center)


def smooth_twice(kappa, source):
    no_shift = (0, 0, 0)
    center = window(kappa, 1, no_shift)
    faces = [face_weight(center, window(kappa, 1, offset)) for offset in NEIGHBOUR_STEPS]
    diagonal = faces[0] + faces[1] + faces[2] + faces[3] + faces[4] + faces[5]
    guarded = jnp.where(center > 0.0, diagonal, 1.0)
    first_sweep = JACOBI_WEIGHT * window(source, 1, no_shift) / guarded
    inner_first = window(first_sweep, 1, no_shift)
    inner_diagonal = window(diagonal, 1, no_shift)
    coupled = jnp.zeros_like(inner_first)
    for face_value, offset in zip(faces, NEIGHBOUR_STEPS):
        coupled = coupled + window(face_value, 1, no_shift) * window(first_sweep, 1, offset)
    residual = window(source, 2, no_shift) - inner_diagonal * inner_first + coupled
    return inner_first + JACOBI_WEIGHT * residual / inner_diagonal


def pad_depth(values):
    return jnp.pad(values, ((0, 0), (0, 0), (2, 2)))


def plain_body(noise, source):
    row_at = lax.axis_index("row")
    group_at = lax.axis_index(("level", "col"))
    fine_field = noise.astype(jnp.float32)
    fine_len = fine_field.shape[-1]
    coarse_len = fine_len // 2
    half_coarse = coarse_len // 2
    kept_modes = fine_len // 2
    real_part, imag_part = forward_axis(fine_field, None, "pq", "pjiq", kept_modes)
    real_part, imag_part = (
        lax.all_to_all(real_part, ("level", "col"), split_axis=1, concat_axis=2, tiled=True),
        lax.all_to_all(imag_part, ("level", "col"), split_axis=1, concat_axis=2, tiled=True),
    )
    real_part, imag_part = forward_axis(real_part, imag_part, "pq", "jiqp", fine_len)
    real_part, imag_part = (
        lax.all_to_all(real_part, "row", split_axis=0, concat_axis=2, tiled=True),
        lax.all_to_all(imag_part, "row", split_axis=0, concat_axis=2, tiled=True),
    )
    slab_len = real_part.shape[-1]
    coarse_slab = slab_len // 2
    half_slab = coarse_slab // 2
    real_part, imag_part = forward_axis(real_part, imag_part, "pq", "pqji", slab_len)
    second_count = real_part.shape[0]
    third_count = real_part.shape[1]
    wave_second = signed_modes(
        row_at * second_count + jnp.arange(second_count, dtype=jnp.int32), fine_len
    )[:, None, None]
    third_index = group_at * third_count + jnp.arange(third_count, dtype=jnp.int32)
    wave_third = signed_modes(third_index, fine_len)[None, :, None]
    spread = 2.0
    mirror_weight = jnp.where(third_index == 0, 1.0, spread).astype(jnp.float32)[None, :, None]
    norm_factor = (float(slab_len) * float(fine_len) * float(fine_len)) ** (-0.5)
    wave_first = signed_modes(jnp.arange(slab_len, dtype=jnp.int32), slab_len)[None, None, :]
    fine_scale = (
        amplitude(
            wave_second, wave_third, wave_first, fine_len / 2.0, fine_len / 2.0, slab_len / 2.0
        )
        * mirror_weight
        * norm_factor
    )
    coarse_first = signed_modes(jnp.arange(coarse_slab, dtype=jnp.int32), coarse_slab)[
        None, None, :
    ]
    coarse_scale = (
        amplitude(
            wave_second,
            wave_third,
            coarse_first,
            coarse_len / 2.0,
            coarse_len / 2.0,
            coarse_slab / 2.0,
        )
        * mirror_weight
        * norm_factor
    )
    coarse_real = low_band(real_part, half_slab, slab_len) * coarse_scale
    coarse_imag = low_band(imag_part, half_slab, slab_len) * coarse_scale
    fine_real, fine_imag = inverse_axis(
        real_part * fine_scale, imag_part * fine_scale, slab_len, "pq", "abqp", False
    )
    coarse_real, coarse_imag = inverse_axis(
        coarse_real, coarse_imag, coarse_slab, "pq", "abqp", False
    )
    fine_real, fine_imag, coarse_real, coarse_imag = (
        lax.all_to_all(fine_real, "row", split_axis=0, concat_axis=2, tiled=True),
        lax.all_to_all(fine_imag, "row", split_axis=0, concat_axis=2, tiled=True),
        lax.all_to_all(coarse_real, "row", split_axis=0, concat_axis=2, tiled=True),
        lax.all_to_all(coarse_imag, "row", split_axis=0, concat_axis=2, tiled=True),
    )
    coarse_real = low_band(coarse_real, half_coarse, fine_len)
    coarse_imag = low_band(coarse_imag, half_coarse, fine_len)
    fine_real, fine_imag = inverse_axis(fine_real, fine_imag, fine_len, "pq", "pabq", False)
    coarse_real, coarse_imag = inverse_axis(
        coarse_real, coarse_imag, coarse_len, "pq", "pabq", False
    )
    fine_real, fine_imag, coarse_real, coarse_imag = (
        lax.all_to_all(fine_real, ("level", "col"), split_axis=1, concat_axis=2, tiled=True),
        lax.all_to_all(fine_imag, ("level", "col"), split_axis=1, concat_axis=2, tiled=True),
        lax.all_to_all(coarse_real, ("level", "col"), split_axis=1, concat_axis=2, tiled=True),
        lax.all_to_all(coarse_imag, ("level", "col"), split_axis=1, concat_axis=2, tiled=True),
    )
    coarse_real = coarse_real[:, :, :half_coarse]
    coarse_imag = coarse_imag[:, :, :half_coarse]
    fine_log = inverse_axis(fine_real, fine_imag, fine_len, "pq", "pqab", True)
    coarse_log = inverse_axis(coarse_real, coarse_imag, coarse_len, "pq", "pqab", True)
    fine_kappa = jnp.exp(fine_log)
    coarse_kappa = jnp.exp(coarse_log)
    fine_source = source.astype(jnp.float32)
    coarse_rows = coarse_log.shape[0]
    coarse_cols = coarse_log.shape[1]
    coarse_source = fine_source.reshape(coarse_rows, 2, coarse_cols, 2, coarse_len, 2).mean(
        axis=(1, 3, 5)
    )
    fine_kappa, fine_source, coarse_kappa, coarse_source = (
        padded(fine_kappa, (("row", 0), (("level", "col"), 1)), 2),
        padded(fine_source, (("row", 0), (("level", "col"), 1)), 2),
        padded(coarse_kappa, (("row", 0), (("level", "col"), 1)), 2),
        padded(coarse_source, (("row", 0), (("level", "col"), 1)), 2),
    )
    fine_pressure = smooth_twice(pad_depth(fine_kappa), pad_depth(fine_source))
    coarse_pressure = smooth_twice(pad_depth(coarse_kappa), pad_depth(coarse_source))
    return (fine_pressure, coarse_pressure)


def body(noise, source):
    planes, cells, length = noise.shape
    rows, groups = lax.axis_size("row"), lax.axis_size(PLANE)
    modes = length // 2 // (rows * groups)
    fills = planes == SUB and cells == LANE and 2 * HALO * modes == LANE // 2
    if fills and length % (4 * LANE) == 0 and rows % 2 == 0 and groups % 4 == 0:
        return fused_body(noise, source)
    return plain_body(noise, source)


def solution(mesh):
    return jax.shard_map(
        body,
        mesh=mesh,
        in_specs=(P("row", ("level", "col"), None), P("row", ("level", "col"), None)),
        out_specs=(P("row", ("level", "col"), None), P("row", ("level", "col"), None)),
        check_vma=False,
    )
```

profile of v0, /device:TPU:1, one launch (start us, length us, event | category | flops | bytes accessed | tf_op | source)
XLA Modules:
  0.0 151.0 jit_solution(7752172799796936772)
XLA Ops:
  0.6 4.6 %shard_map.212 = f32[4096,128]{1,0:T(8,128)} custom-call(bf16[4,256,512]{2,1,0:T(8,128)(2,1)} %constant.80.clone.d_hbm, bf16[1024,512]{1,0:T(8,128)(2,1)} %bitcast.19), custom_call_target="tpu_custom_call" | custom-call | flops 1073741824 | bytes 4194304 | tf_op jit(solution)/shard_map/pallas_call | solution.py:768
  5.3 7.1 %all-to-all-start = ((f32[32,16,8,128]{3,2,1,0:T(8,128)}), f32[32,16,8,128]{3,2,1,0:T(8,128)S(1)}, u32[]{:S(2)}, u32[]{:S(2)}) async-start(f32[32,16,8,128]{3,2,1,0:T(8,128)} %bitcast.18), calls=%async_computation | async-start | bytes 4194304 | tf_op jit(solution)/shard_map/all_to_all | solution.py:857
  12.4 1.3 shard_map.213
  13.7 0.7 copy-done.6
  14.4 3.5 %collective-permute-start = (f32[160,512]{1,0:T(8,128)}, f32[160,512]{1,0:T(8,128)S(1)}, u32[]{:S(2)}, u32[]{:S(2)}) collective-permute-start(f32[160,512]{1,0:T(8,128)} %get-tuple-element.45), channel_id=1, source_target_pairs={{0,2},{2,4},{4,6},{6,8},{8,10},{10,12},{12,14},{1,3},{3,5},{5,7},{... | collective-permute-start | bytes 983048 | tf_op jit(solution)/shard_map/ppermute | solution.py:795
  17.9 1.9 %collective-permute-start.1 = (f32[160,512]{1,0:T(8,128)}, f32[160,512]{1,0:T(8,128)S(1)}, u32[]{:S(2)}, u32[]{:S(2)}) collective-permute-start(f32[160,512]{1,0:T(8,128)} %get-tuple-element.46), channel_id=1, source_target_pairs={{2,0},{4,2},{6,4},{8,6},{10,8},{12,10},{14,12},{3,1},{5,3},{7,5},{... | collective-permute-start | bytes 983048 | tf_op jit(solution)/shard_map/ppermute | solution.py:795
  19.9 3.1 %collective-permute-start.2 = (f32[16,512]{1,0:T(8,128)S(1)}, f32[16,512]{1,0:T(8,128)S(1)}, u32[]{:S(2)}, u32[]{:S(2)}) collective-permute-start(f32[16,512]{1,0:T(8,128)S(1)} %get-tuple-element.47), channel_id=1, source_target_pairs={{0,1},{1,16},{16,17},{2,3},{3,18},{18,19},{4,5},{5,20},{20,21},{6,... | collective-permute-start | bytes 98312 | tf_op jit(solution)/shard_map/ppermute | solution.py:795
  23.0 1.3 collective-permute-start.3
  24.3 0.1 copy.26.scale
  24.4 4.0 %collective-permute-done.3.rest_5_ = f32[16,512]{1,0:T(8,128)S(1)} collective-permute-done((f32[16,512]{1,0:T(8,128)S(1)}, f32[16,512]{1,0:T(8,128)S(1)}, u32[]{:S(2)}, u32[]{:S(2)}) %collective-permute-start.3) | collective-permute-done | bytes 32800 | tf_op jit(solution)/shard_map/ppermute | solution.py:795
  28.4 22.1 %collective-permute-done.rest_2_ = f32[160,512]{1,0:T(8,128)S(1)} collective-permute-done((f32[160,512]{1,0:T(8,128)}, f32[160,512]{1,0:T(8,128)S(1)}, u32[]{:S(2)}, u32[]{:S(2)}) %collective-permute-start) | collective-permute-done | bytes 327712 | tf_op jit(solution)/shard_map/ppermute | solution.py:795
  50.5 10.0 %all-to-all-done.b = f32[32,16,8,128]{3,2,1,0:T(8,128)S(1)} async-done(((f32[32,16,8,128]{3,2,1,0:T(8,128)}), f32[32,16,8,128]{3,2,1,0:T(8,128)S(1)}, u32[]{:S(2)}, u32[]{:S(2)}) %all-to-all-start) | async-done | bytes 2097184 | tf_op jit(solution)/shard_map/all_to_all | solution.py:857
  60.5 7.3 %shard_map.214 = f32[32,19,8,128]{3,2,1,0:T(8,128)} custom-call(f32[8,2]{1,0:T(8,128)S(1)} %copy.26.scale, f32[32,16,8,128]{3,2,1,0:T(8,128)S(1)} %all-to-all-done.b, bf16[2,256,256]{2,1,0:T(8,128)(2,1)} %constant.83.clone.rest_0_, bf16[2,256,256]{2,1,0:T(8,128)(2,1)} %constant.84.clone.rest_1_, bf16[256,256]{1,0:T(8,128)(2,1)} %constant.85.clone.rest_2_, ...), custom_call_target="tpu_custom_call" | custom-call | flops 4026531840 | bytes 7012416 | tf_op jit(solution)/shard_map/pallas_call | solution.py:768
  67.9 6.9 %all-to-all-start.1 = ((f32[32,19,8,128]{3,2,1,0:T(8,128)}), f32[32,19,8,128]{3,2,1,0:T(8,128)S(1)}, u32[]{:S(2)}, u32[]{:S(2)}) async-start(f32[32,19,8,128]{3,2,1,0:T(8,128)} %shard_map.214), calls=%async_computation.1 | async-start | bytes 4980736 | tf_op jit(solution)/shard_map/all_to_all | solution.py:918
  74.8 0.1 stack.32
  74.9 1.7 %shard_map.215 = (f32[6,4,144,128]{3,2,1,0:T(8,128)S(1)}, f32[2,2,4,144,128]{4,3,2,1,0:T(8,128)S(1)}, f32[2,2,80,128]{3,2,1,0:T(8,128)S(1)}, f32[2,2,2,80,128]{4,3,2,1,0:T(8,128)S(1)}) custom-call(bf16[8,128,512]{2,1,0:T(8,128)(2,1)} %rest_0_.2, f32[4,64,256]{2,1,0:T(8,128)} %bitcast.17, f32[160,512]{1,0:T(8,128)} %copy-done.7, f32[160,512]{1,0:T(8,128)} %copy-done.8, ...), custom_call_target="tpu_custom_call" | custom-call | flops 524288 | bytes 5472256 | tf_op jit(solution)/shard_map/pallas_call | solution.py:768
  76.7 1.2 copy-done.1
  77.9 1.0 copy-done.3
  78.9 52.5 %all-to-all-done.1 = f32[32,19,8,128]{3,2,1,0:T(8,128)S(1)} async-done(((f32[32,19,8,128]{3,2,1,0:T(8,128)}), f32[32,19,8,128]{3,2,1,0:T(8,128)S(1)}, u32[]{:S(2)}, u32[]{:S(2)}) %all-to-all-start.1) | async-done | bytes 2490400 | tf_op jit(solution)/shard_map/all_to_all | solution.py:918
  131.4 3.7 %shard_map.216 = (f32[4,4,144,128]{3,2,1,0:T(8,128)S(1)}, f32[4,2,80,128]{3,2,1,0:T(8,128)S(1)}, f32[32,512]{1,0:T(8,128)S(1)}, f32[1296,128]{1,0:T(8,128)S(1)}, f32[1296,128]{1,0:T(8,128)S(1)}) custom-call(s32[5]{0:T(128)S(1)} %convert_element_type.6.flags, f32[4864,128]{1,0:T(8,128)S(1)} %bitcast.14, bf16[2,256,256]{2,1,0:T(8,128)(2,1)} %constant.92.clone.rest_0_.eh_hbm, ...), custom_call_target="tpu_custom_call" | custom-call | flops 805306368 | bytes 6471700 | tf_op jit(solution)/shard_map/pallas_call | solution.py:768
  135.1 3.5 %collective-permute-start.4 = (f32[1296,128]{1,0:T(8,128)S(1)}, f32[1296,128]{1,0:T(8,128)S(1)}, u32[]{:S(2)}, u32[]{:S(2)}) collective-permute-start(f32[1296,128]{1,0:T(8,128)S(1)} %get-tuple-element.81), channel_id=1, source_target_pairs={{2,4},{4,2},{6,8},{8,6},{10,12},{12,10},{3,5},{5,3},{7,9},{9,7},{1... | collective-permute-start | bytes 1990664 | tf_op jit(solution)/shard_map/ppermute | solution.py:960
  138.7 6.2 %shard_map.217 = (f32[8,128,512]{2,1,0:T(8,128)}, f32[6,4,144,128]{3,2,1,0:T(8,128)S(1)}, f32[6,4,144,128]{3,2,1,0:T(8,128)S(1)}, f32[6,4,144,128]{3,2,1,0:T(8,1...) custom-call(s32[5]{0:T(128)S(1)} %convert_element_type.6.flags, ...), custom_call_target="tpu_custom_call" | custom-call | flops 805306368 | bytes 14417940 | tf_op jit(solution)/shard_map/pallas_call | solution.py:768
  144.9 2.1 %collective-permute-done.4.rest_10_ = f32[1296,128]{1,0:T(8,128)S(1)} collective-permute-done((f32[1296,128]{1,0:T(8,128)S(1)}, f32[1296,128]{1,0:T(8,128)S(1)}, u32[]{:S(2)}, u32[]{:S(2)}) %collective-permute-start.4) | collective-permute-done | bytes 663584 | tf_op jit(solution)/shard_map/ppermute | solution.py:960
  147.1 3.9 %shard_map.218 = (f32[8,128,512]{2,1,0:T(8,128)}, f32[4,64,256]{2,1,0:T(8,128)}) custom-call(s32[5]{0:T(128)S(1)} %convert_element_type.6.flags, f32[4,4,144,128]{3,2,1,0:T(8,128)S(1)} %get-tuple-element.68.edges.rest_0_, f32[2,2,4,144,128]{4,3,2,1,0:T(8,128)S(1)} %copy-done.4, ...), custom_call_target="tpu_custom_call", output_to_operand_aliasing={{0}: (13, {})} | custom-call | flops 15728640 | bytes 14598164 | tf_op jit(solution)/shard_map/pallas_call | solution.py:768
  (26 shorter events, 0.1 us)
Async XLA Ops:
  5.3 7.1 %copy-start = (bf16[8,128,512]{2,1,0:T(8,128)(2,1)S(1)}, bf16[8,128,512]{2,1,0:T(8,128)(2,1)}, u32[]{:S(2)}) copy-start(bf16[8,128,512]{2,1,0:T(8,128)(2,1)} %rest_0_.2) | copy-start | bytes 3145732
  5.3 7.1 %copy-start.5 = (bf16[512,256]{1,0:T(8,128)(2,1)S(1)}, bf16[512,256]{1,0:T(8,128)(2,1)}, u32[]{:S(2)}) copy-start(bf16[512,256]{1,0:T(8,128)(2,1)} %constant.81.clone.pairs) | copy-start | bytes 786436
  5.3 55.2 %all-to-all-start = ((f32[32,16,8,128]{3,2,1,0:T(8,128)}), f32[32,16,8,128]{3,2,1,0:T(8,128)S(1)}, u32[]{:S(2)}, u32[]{:S(2)}) async-start(f32[32,16,8,128]{3,2,1,0:T(8,128)} %bitcast.18), calls=%async_computation | async-start | bytes 4194304 | tf_op jit(solution)/shard_map/all_to_all | solution.py:857
  13.7 0.7 copy-start.6
  14.4 36.1 %collective-permute-start = (f32[160,512]{1,0:T(8,128)}, f32[160,512]{1,0:T(8,128)S(1)}, u32[]{:S(2)}, u32[]{:S(2)}) collective-permute-start(f32[160,512]{1,0:T(8,128)} %get-tuple-element.45), channel_id=1, source_target_pairs={{0,2},{2,4},{4,6},{6,8},{8,10},{10,12},{12,14},{1,3},{3,5},{5,7},{... | collective-permute-start | bytes 983048 | tf_op jit(solution)/shard_map/ppermute | solution.py:795
  17.9 32.6 %collective-permute-start.1 = (f32[160,512]{1,0:T(8,128)}, f32[160,512]{1,0:T(8,128)S(1)}, u32[]{:S(2)}, u32[]{:S(2)}) collective-permute-start(f32[160,512]{1,0:T(8,128)} %get-tuple-element.46), channel_id=1, source_target_pairs={{2,0},{4,2},{6,4},{8,6},{10,8},{12,10},{14,12},{3,1},{5,3},{7,5},{... | collective-permute-start | bytes 983048 | tf_op jit(solution)/shard_map/ppermute | solution.py:795
  19.9 4.5 %collective-permute-start.2 = (f32[16,512]{1,0:T(8,128)S(1)}, f32[16,512]{1,0:T(8,128)S(1)}, u32[]{:S(2)}, u32[]{:S(2)}) collective-permute-start(f32[16,512]{1,0:T(8,128)S(1)} %get-tuple-element.47), channel_id=1, source_target_pairs={{0,1},{1,16},{16,17},{2,3},{3,18},{18,19},{4,5},{5,20},{20,21},{6,... | collective-permute-start | bytes 98312 | tf_op jit(solution)/shard_map/ppermute | solution.py:795
  23.0 5.5 %collective-permute-start.3 = (f32[16,512]{1,0:T(8,128)S(1)}, f32[16,512]{1,0:T(8,128)S(1)}, u32[]{:S(2)}, u32[]{:S(2)}) collective-permute-start(f32[16,512]{1,0:T(8,128)S(1)} %get-tuple-element.48), channel_id=1, source_target_pairs={{1,0},{16,1},{17,16},{3,2},{18,3},{19,18},{5,4},{20,5},{21,20},{7,... | collective-permute-start | bytes 98312 | tf_op jit(solution)/shard_map/ppermute | solution.py:795
  24.4 43.5 %copy-start.9 = (f32[16,512]{1,0:T(8,128)}, f32[16,512]{1,0:T(8,128)S(1)}, u32[]{:S(2)}) copy-start(f32[16,512]{1,0:T(8,128)S(1)} %collective-permute-done.2.rest_4_) | copy-start | bytes 98308
  28.4 39.5 %copy-start.10 = (f32[16,512]{1,0:T(8,128)}, f32[16,512]{1,0:T(8,128)S(1)}, u32[]{:S(2)}) copy-start(f32[16,512]{1,0:T(8,128)S(1)} %collective-permute-done.3.rest_5_) | copy-start | bytes 98308
  50.5 17.4 %copy-start.7 = (f32[160,512]{1,0:T(8,128)}, f32[160,512]{1,0:T(8,128)S(1)}, u32[]{:S(2)}) copy-start(f32[160,512]{1,0:T(8,128)S(1)} %collective-permute-done.rest_2_) | copy-start | bytes 983044
  50.5 17.4 %copy-start.8 = (f32[160,512]{1,0:T(8,128)}, f32[160,512]{1,0:T(8,128)S(1)}, u32[]{:S(2)}) copy-start(f32[160,512]{1,0:T(8,128)S(1)} %collective-permute-done.1.rest_3_) | copy-start | bytes 983044
  67.9 63.5 %all-to-all-start.1 = ((f32[32,19,8,128]{3,2,1,0:T(8,128)}), f32[32,19,8,128]{3,2,1,0:T(8,128)S(1)}, u32[]{:S(2)}, u32[]{:S(2)}) async-start(f32[32,19,8,128]{3,2,1,0:T(8,128)} %shard_map.214), calls=%async_computation.1 | async-start | bytes 4980736 | tf_op jit(solution)/shard_map/all_to_all | solution.py:918
  76.7 1.2 copy-start.1
  77.9 1.0 copy-start.3
  131.4 7.3 %copy-start.2 = (f32[6,4,144,128]{3,2,1,0:T(8,128)S(1)}, f32[6,4,144,128]{3,2,1,0:T(8,128)}, u32[]{:S(2)}) copy-start(f32[6,4,144,128]{3,2,1,0:T(8,128)} %copy-done.1) | copy-start | bytes 5308420
  135.1 12.0 %collective-permute-start.4 = (f32[1296,128]{1,0:T(8,128)S(1)}, f32[1296,128]{1,0:T(8,128)S(1)}, u32[]{:S(2)}, u32[]{:S(2)}) collective-permute-start(f32[1296,128]{1,0:T(8,128)S(1)} %get-tuple-element.81), channel_id=1, source_target_pairs={{2,4},{4,2},{6,8},{8,6},{10,12},{12,10},{3,5},{5,3},{7,9},{9,7},{1... | collective-permute-start | bytes 1990664 | tf_op jit(solution)/shard_map/ppermute | solution.py:960
  138.6 8.5 %collective-permute-start.5 = (f32[1296,128]{1,0:T(8,128)S(1)}, f32[1296,128]{1,0:T(8,128)S(1)}, u32[]{:S(2)}, u32[]{:S(2)}) collective-permute-start(f32[1296,128]{1,0:T(8,128)S(1)} %get-tuple-element.82), channel_id=1, source_target_pairs={{0,2},{2,0},{4,6},{6,4},{8,10},{10,8},{12,14},{14,12},{1,3},{3,1},... | collective-permute-start | bytes 1990664 | tf_op jit(solution)/shard_map/ppermute | solution.py:960
  138.7 8.4 %copy-start.4 = (f32[2,2,4,144,128]{4,3,2,1,0:T(8,128)S(1)}, f32[2,2,4,144,128]{4,3,2,1,0:T(8,128)}, u32[]{:S(2)}) copy-start(f32[2,2,4,144,128]{4,3,2,1,0:T(8,128)} %copy-done.3) | copy-start | bytes 3538948
where the time goes:
time: 151 us
  waiting for transfers between devices  90.7 us (60%)
  Pallas kernels  28.8 us (19%)
  starting transfers between devices  27.4 us (18%)
  local copies, waits for them, and re-layouts  3.15 us (2%)
    all_to_all x1, waiting for transfers between devices, fused_body(): got = lax.all_to_all(out, EVERY, split_axis=0, concat_axis=0, tiled=True)  52.5 us
    pallas_call x7, Pallas kernels, call(): pl.pallas_call(kernel, out_shape=outs, in_specs=specs, out_specs=out_spec...  28.8 us
    ppermute x4, waiting for transfers between devices, swap(): return (lax.ppermute(hi, axis, up), lax.ppermute(lo, axis, down))  26.1 us
    all_to_all x1, waiting for transfers between devices, fused_body(): lax.all_to_all(sent, EVERY, split_axis=0, concat_axis=0, tiled=True)  9.98 us
    ppermute x4, starting transfers between devices, swap(): return (lax.ppermute(hi, axis, up), lax.ppermute(lo, axis, down))  9.83 us
    all_to_all x1, starting transfers between devices, fused_body(): lax.all_to_all(sent, EVERY, split_axis=0, concat_axis=0, tiled=True)  7.1 us
    all_to_all x1, starting transfers between devices, fused_body(): got = lax.all_to_all(out, EVERY, split_axis=0, concat_axis=0, tiled=True)  6.9 us
    ppermute x2, starting transfers between devices, fused_body(): lax.ppermute(x, 'row', [p for i in range(at, rows - 1, 2) for p in ((i, i...  3.61 us
  transfers between devices with their start and end apart: 8, of which 5 were waited for; matrix products, arithmetic and copies ran while one was open for 0% of the time, Pallas kernels for 6%

commit v1 on v0

--- a/solution.py
+++ b/solution.py
@@ -474,7 +474,7 @@
     return SUB - 2 + h if h < 2 else SUB + cells + h - 2
 
 
-def source_kernel(planes, pairs, x, out, lo, hi, left, right, held, summed):
+def source_kernel(planes, flags, pairs, x, out, far, near, left, right, held, summed):
     cells = x.shape[0] // planes
     length = x.shape[1]
     half, fourth = cells // 2, cells // 4
@@ -487,11 +487,17 @@
             out[n * half : (n + 1) * half, lanes] = (
                 summed[pl.ds(0, half, stride=2), :] + summed[pl.ds(1, half, stride=2), :]
             )
-    for edge, plane in ((lo, 0), (hi, planes - 1)):
-        edge[:cells, :] = x[plane * cells : (plane + 1) * cells, :].astype(jnp.float32)
-        at = plane // 2 * half
-        edge[cells:, : length // 2] = out[at : at + fourth, :]
-        edge[cells:, length // 2 :] = out[at + fourth : at + half, :]
+    odd_row = flags[4] == 1
+    ends = (0, planes - 1)
+    for edge, plane in (
+        (far, jnp.where(odd_row, ends[1], ends[0])),
+        (near, jnp.where(odd_row, ends[0], ends[1])),
+    ):
+        at = pl.multiple_of(plane * cells, cells)
+        edge[:cells, :] = x[pl.ds(at, cells), :].astype(jnp.float32)
+        at = pl.multiple_of(lax.div(plane, 2) * half, half)
+        edge[cells:, : length // 2] = out[pl.ds(at, fourth), :]
+        edge[cells:, length // 2 :] = out[pl.ds(at + fourth, fourth), :]
     for edge, row in ((left, 0), (right, cells - 1)):
         edge[...] = jnp.zeros_like(edge)
         for n in range(planes):
@@ -584,7 +590,7 @@
         put_rows(held, to, SUB + half, source[row : row + half, length:])
 
 
-def layout_kernel(sizes, *rest):
+def layout_kernel(sizes, flags, *rest):
     away, outs, near, sems = rest[:6], rest[6:10], rest[10:16], rest[16]
     for copy in load(list(zip(away, near)), sems):
         copy.wait()
@@ -603,9 +609,10 @@
 
         for p in range(1, planes - 1):
             plane(inner, p - 1, p)
+        row = 0 if fine else 2 * cells
+        for group, edge in ((flags[4], edges[0]), (1 - flags[4], edges[1])):
+            put_block(fine, outer.at[group], 0, edge, row, cells, length)
         for group, p in enumerate((0, planes - 1)):
-            row = 0 if fine else 2 * cells
-            put_block(fine, outer.at[group], 0, edges[group], row, cells, length)
             plane(outer.at[group], 1, p)
 
 
@@ -795,6 +802,12 @@
     return lax.ppermute(hi, axis, up), lax.ppermute(lo, axis, down)
 
 
+def trade(x, start):
+    rows = lax.axis_size("row")
+    pairs = [p for i in range(start, rows - 1, 2) for p in ((i, i + 1), (i + 1, i))]
+    return lax.ppermute(x, "row", pairs)
+
+
 def held_planes(size, *count):
     planes, cells, length = size
     return f32(*count, length // LANE, cells + 2 * SUB, LANE)
@@ -863,18 +876,22 @@
     coarse_source, *edges = call(
         functools.partial(source_kernel, planes),
         [f32(planes * cells // 4, length // 2), level, level, side, side],
-        (pairs.astype(bf16), source.reshape(flat)),
+        (flags, pairs.astype(bf16), source.reshape(flat)),
         [
             pltpu.VMEM((planes * cells, length // 2), jnp.float32),
             pltpu.VMEM((cells, LANE), jnp.float32),
         ],
         planes * cells * length * length,
-        [VMEM] * 2,
+        [SMEM] + [VMEM] * 2,
         12,
     )
     coarse_source = coarse_source.reshape(planes // 2, cells // 2, length // 2)
-    edges = (*swap(*edges[:2], "row"), *swap(*edges[2:], PLANE))
-    arrived, edges, coarse_source = lax.optimization_barrier((arrived, edges, coarse_source))
+    far, near, *sides = edges
+    near, sides = trade(near, 0), swap(*sides, PLANE)
+    arrived, far, near, sides, coarse_source = lax.optimization_barrier(
+        (arrived, far, near, sides, coarse_source)
+    )
+    edges = (trade(far, 1), near, *sides)
 
     constants = (
         two_parts(second_table(second))
@@ -926,10 +943,10 @@
             for s in sizes
             for count in ((s[0] - 2,), (2, 2))
         ],
-        sources,
+        (flags, *sources),
         room(*sources) + [pltpu.SemaphoreType.DMA((6,))],
         source.size,
-        [AWAY] * 6,
+        [SMEM] + [AWAY] * 6,
         12,
     )
     got, laid = lax.optimization_barrier((got, laid))
@@ -956,12 +973,7 @@
         [SMEM, VMEM] + [AWAY] * 7,
         16,
     )
-    k_far, k_near = (
-        lax.ppermute(
-            x, "row", [p for i in range(at, rows - 1, 2) for p in ((i, i + 1), (i + 1, i))]
-        )
-        for x, at in ((far, 1), (near, 0))
-    )
+    k_far, k_near = trade(far, 1), trade(near, 0)
     inner_f, outer_f, coarse_inner_f, coarse_outer_f = laid
     inner, *kept = call(
         functools.partial(inner_kernel, size, shares),

time: 151 us -> 152 us (level)
  starting transfers between devices: 27.4 us -> 22.1 us
  waiting for transfers between devices: 90.7 us -> 93.8 us
    all_to_all x1, waiting for transfers between devices: 9.98 us -> 35.8 us  [fused_body(): lax.all_to_all(sent, EVERY, split_axis=0, concat_axis=0, tiled=True)]
    ppermute x4 -> x2, waiting for transfers between devices: 26.1 us -> 3.88 us  [swap(): return (lax.ppermute(hi, axis, up), lax.ppermute(lo, axis, down))]
    ppermute x4 -> x2, starting transfers between devices: 9.83 us -> 4.68 us  [swap(): return (lax.ppermute(hi, axis, up), lax.ppermute(lo, axis, down))]
    all_to_all x1, starting transfers between devices: 6.9 us -> 2.57 us  [fused_body(): got = lax.all_to_all(out, EVERY, split_axis=0, concat_axis=0, tiled=True)]
    ppermute x2 -> x4, starting transfers between devices: 3.61 us -> 7.75 us  [trade(): return lax.ppermute(x, 'row', pairs)]
    unnamed x22 -> x24, local copies, waits for them, and re-layouts: 2.96 us -> 4.41 us
  transfers between devices with their start and end apart: 8 -> 8, of which waited for: 5 -> 4; matrix products, arithmetic and copies ran while one was open for 0% -> 0% of each run, Pallas kernels for 6% -> 12%
where the time goes in v1:
time: 152 us
  waiting for transfers between devices  93.8 us (62%)
  Pallas kernels  30.2 us (20%)
  starting transfers between devices  22.1 us (15%)
  local copies, waits for them, and re-layouts  4.6 us (3%)
    all_to_all x1, waiting for transfers between devices, fused_body(): got = lax.all_to_all(out, EVERY, split_axis=0, concat_axis=0, tiled=True)  52 us
    all_to_all x1, waiting for transfers between devices, fused_body(): lax.all_to_all(sent, EVERY, split_axis=0, concat_axis=0, tiled=True)  35.8 us
    pallas_call x7, Pallas kernels, call(): pl.pallas_call(kernel, out_shape=outs, in_specs=specs, out_specs=out_spec...  30.2 us
    ppermute x4, starting transfers between devices, trade(): return lax.ppermute(x, 'row', pairs)  7.75 us
    all_to_all x1, starting transfers between devices, fused_body(): lax.all_to_all(sent, EVERY, split_axis=0, concat_axis=0, tiled=True)  7.1 us
    ppermute x2, starting transfers between devices, swap(): return (lax.ppermute(hi, axis, up), lax.ppermute(lo, axis, down))  4.68 us
    unnamed x24, local copies, waits for them, and re-layouts  4.41 us
    ppermute x2, waiting for transfers between devices, swap(): return (lax.ppermute(hi, axis, up), lax.ppermute(lo, axis, down))  3.88 us
  transfers between devices with their start and end apart: 8, of which 4 were waited for; matrix products, arithmetic and copies ran while one was open for 0% of the time, Pallas kernels for 12%

profile of v1, /device:TPU:1, one launch (start us, length us, event | category | flops | bytes accessed | tf_op | source)
XLA Modules:
  0.0 151.5 jit_solution(6040156835901327957)
XLA Ops:
  0.6 4.6 %shard_map.212 = f32[4096,128]{1,0:T(8,128)} custom-call(bf16[4,256,512]{2,1,0:T(8,128)(2,1)} %constant.80.clone.d_hbm, bf16[1024,512]{1,0:T(8,128)(2,1)} %bitcast.19), custom_call_target="tpu_custom_call" | custom-call | flops 1073741824 | bytes 4194304 | tf_op jit(solution)/shard_map/pallas_call | solution.py:775
  5.3 7.1 %all-to-all-start = ((f32[32,16,8,128]{3,2,1,0:T(8,128)}), f32[32,16,8,128]{3,2,1,0:T(8,128)S(1)}, u32[]{:S(2)}, u32[]{:S(2)}) async-start(f32[32,16,8,128]{3,2,1,0:T(8,128)} %bitcast.18), calls=%async_computation | async-start | bytes 4194304 | tf_op jit(solution)/shard_map/all_to_all | solution.py:870
  12.4 0.1 stack.32
  12.5 1.8 %shard_map.213 = (f32[256,256]{1,0:T(8,128)S(1)}, f32[160,512]{1,0:T(8,128)S(1)}, f32[160,512]{1,0:T(8,128)}, f32[16,512]{1,0:T(8,128)S(1)}, f32[16,512]{1,0:T(8,128)S(1)}) custom-call(s32[5]{0:T(128)S(1)} %convert_element_type.6.flags, bf16[512,256]{1,0:T(8,128)(2,1)S(1)} %copy-done.5, bf16[1024,512]{1,0:T(8,128)(2,1)S(1)} %bitcast.16), custom_call_target="tpu_custom_call" | custom-call | flops 268435456 | bytes 2293780 | tf_op jit(solution)/shard_map/pallas_call | solution.py:775
  14.3 0.7 copy-done.6
  15.0 0.7 copy-done.7
  15.8 0.3 collective-permute-start
  16.0 3.4 %collective-permute-start.1 = (f32[16,512]{1,0:T(8,128)S(1)}, f32[16,512]{1,0:T(8,128)S(1)}, u32[]{:S(2)}, u32[]{:S(2)}) collective-permute-start(f32[16,512]{1,0:T(8,128)S(1)} %get-tuple-element.47), channel_id=1, source_target_pairs={{0,1},{1,16},{16,17},{2,3},{3,18},{18,19},{4,5},{5,20},{20,21},{6,... | collective-permute-start | bytes 98312 | tf_op jit(solution)/shard_map/ppermute | solution.py:802
  19.4 1.3 collective-permute-start.2
  20.8 3.9 %collective-permute-done.2.rest_5_ = f32[16,512]{1,0:T(8,128)S(1)} collective-permute-done((f32[16,512]{1,0:T(8,128)S(1)}, f32[16,512]{1,0:T(8,128)S(1)}, u32[]{:S(2)}, u32[]{:S(2)}) %collective-permute-start.2) | collective-permute-done | bytes 32800 | tf_op jit(solution)/shard_map/ppermute | solution.py:802
  24.7 35.8 %all-to-all-done.b = f32[32,16,8,128]{3,2,1,0:T(8,128)S(1)} async-done(((f32[32,16,8,128]{3,2,1,0:T(8,128)}), f32[32,16,8,128]{3,2,1,0:T(8,128)S(1)}, u32[]{:S(2)}, u32[]{:S(2)}) %all-to-all-start) | async-done | bytes 2097184 | tf_op jit(solution)/shard_map/all_to_all | solution.py:870
  60.5 3.9 %collective-permute-start.3 = (f32[160,512]{1,0:T(8,128)}, f32[160,512]{1,0:T(8,128)S(1)}, u32[]{:S(2)}, u32[]{:S(2)}) collective-permute-start(f32[160,512]{1,0:T(8,128)} %copy-done.7), channel_id=1, source_target_pairs={{2,4},{4,2},{6,8},{8,6},{10,12},{12,10},{3,5},{5,3},{7,9},{9,7},{1... | collective-permute-start | bytes 983048 | tf_op jit(solution)/shard_map/ppermute | solution.py:808
  64.4 7.4 %shard_map.214 = f32[32,19,8,128]{3,2,1,0:T(8,128)} custom-call(f32[8,2]{1,0:T(8,128)S(1)} %copy.26.scale, f32[32,16,8,128]{3,2,1,0:T(8,128)S(1)} %all-to-all-done.b, bf16[2,256,256]{2,1,0:T(8,128)(2,1)} %constant.83.clone.rest_0_, bf16[2,256,256]{2,1,0:T(8,128)(2,1)} %constant.84.clone.rest_1_, bf16[256,256]{1,0:T(8,128)(2,1)} %constant.85.clone.rest_2_, ...), custom_call_target="tpu_custom_call" | custom-call | flops 4026531840 | bytes 7012416 | tf_op jit(solution)/shard_map/pallas_call | solution.py:775
  71.9 0.7 copy-done.9
  72.6 2.6 %all-to-all-start.1 = ((f32[32,19,8,128]{3,2,1,0:T(8,128)}), f32[32,19,8,128]{3,2,1,0:T(8,128)S(1)}, u32[]{:S(2)}, u32[]{:S(2)}) async-start(f32[32,19,8,128]{3,2,1,0:T(8,128)} %shard_map.214), calls=%async_computation.1 | async-start | bytes 4980736 | tf_op jit(solution)/shard_map/all_to_all | solution.py:935
  75.2 2.3 %shard_map.215 = (f32[6,4,144,128]{3,2,1,0:T(8,128)S(1)}, f32[2,2,4,144,128]{4,3,2,1,0:T(8,128)S(1)}, f32[2,2,80,128]{3,2,1,0:T(8,128)S(1)}, f32[2,2,2,80,128]{4,3,2,1,0:T(8,128)S(1)}) custom-call(s32[5]{0:T(128)S(1)} %convert_element_type.6.flags, bf16[8,128,512]{2,1,0:T(8,128)(2,1)} %rest_0_.2, f32[4,64,256]{2,1,0:T(8,128)} %bitcast.17, ...), custom_call_target="tpu_custom_call" | custom-call | flops 524288 | bytes 5472276 | tf_op jit(solution)/shard_map/pallas_call | solution.py:775
  77.5 1.2 copy-done.1
  78.7 1.0 copy-done.3
  79.7 52.0 %all-to-all-done.1 = f32[32,19,8,128]{3,2,1,0:T(8,128)S(1)} async-done(((f32[32,19,8,128]{3,2,1,0:T(8,128)}), f32[32,19,8,128]{3,2,1,0:T(8,128)S(1)}, u32[]{:S(2)}, u32[]{:S(2)}) %all-to-all-start.1) | async-done | bytes 2490400 | tf_op jit(solution)/shard_map/all_to_all | solution.py:935
  131.8 3.7 %shard_map.216 = (f32[4,4,144,128]{3,2,1,0:T(8,128)S(1)}, f32[4,2,80,128]{3,2,1,0:T(8,128)S(1)}, f32[32,512]{1,0:T(8,128)S(1)}, f32[1296,128]{1,0:T(8,128)S(1)}, f32[1296,128]{1,0:T(8,128)S(1)}) custom-call(s32[5]{0:T(128)S(1)} %convert_element_type.6.flags, f32[4864,128]{1,0:T(8,128)S(1)} %bitcast.14, bf16[2,256,256]{2,1,0:T(8,128)(2,1)} %constant.92.clone.rest_0_.eh_hbm, ...), custom_call_target="tpu_custom_call" | custom-call | flops 805306368 | bytes 6471700 | tf_op jit(solution)/shard_map/pallas_call | solution.py:775
  135.4 3.5 %collective-permute-start.4 = (f32[1296,128]{1,0:T(8,128)S(1)}, f32[1296,128]{1,0:T(8,128)S(1)}, u32[]{:S(2)}, u32[]{:S(2)}) collective-permute-start(f32[1296,128]{1,0:T(8,128)S(1)} %get-tuple-element.81), channel_id=1, source_target_pairs={{2,4},{4,2},{6,8},{8,6},{10,12},{12,10},{3,5},{5,3},{7,9},{9,7},{1... | collective-permute-start | bytes 1990664 | tf_op jit(solution)/shard_map/ppermute | solution.py:808
  139.1 6.3 %shard_map.217 = (f32[8,128,512]{2,1,0:T(8,128)}, f32[6,4,144,128]{3,2,1,0:T(8,128)S(1)}, f32[6,4,144,128]{3,2,1,0:T(8,128)S(1)}, f32[6,4,144,128]{3,2,1,0:T(8,1...) custom-call(s32[5]{0:T(128)S(1)} %convert_element_type.6.flags, ...), custom_call_target="tpu_custom_call" | custom-call | flops 805306368 | bytes 14417940 | tf_op jit(solution)/shard_map/pallas_call | solution.py:775
  145.4 2.1 %collective-permute-done.4.rest_10_ = f32[1296,128]{1,0:T(8,128)S(1)} collective-permute-done((f32[1296,128]{1,0:T(8,128)S(1)}, f32[1296,128]{1,0:T(8,128)S(1)}, u32[]{:S(2)}, u32[]{:S(2)}) %collective-permute-start.4) | collective-permute-done | bytes 663584 | tf_op jit(solution)/shard_map/ppermute | solution.py:808
  147.4 4.1 %shard_map.218 = (f32[8,128,512]{2,1,0:T(8,128)}, f32[4,64,256]{2,1,0:T(8,128)}) custom-call(s32[5]{0:T(128)S(1)} %convert_element_type.6.flags, f32[4,4,144,128]{3,2,1,0:T(8,128)S(1)} %get-tuple-element.68.edges.rest_0_, f32[2,2,4,144,128]{4,3,2,1,0:T(8,128)S(1)} %copy-done.4, ...), custom_call_target="tpu_custom_call", output_to_operand_aliasing={{0}: (13, {})} | custom-call | flops 15728640 | bytes 14598164 | tf_op jit(solution)/shard_map/pallas_call | solution.py:775
  (28 shorter events, 0.2 us)
Async XLA Ops:
  5.3 7.3 %copy-start = (bf16[8,128,512]{2,1,0:T(8,128)(2,1)S(1)}, bf16[8,128,512]{2,1,0:T(8,128)(2,1)}, u32[]{:S(2)}) copy-start(bf16[8,128,512]{2,1,0:T(8,128)(2,1)} %rest_0_.2) | copy-start | bytes 3145732
  5.3 7.3 %copy-start.5 = (bf16[512,256]{1,0:T(8,128)(2,1)S(1)}, bf16[512,256]{1,0:T(8,128)(2,1)}, u32[]{:S(2)}) copy-start(bf16[512,256]{1,0:T(8,128)(2,1)} %constant.81.clone.pairs) | copy-start | bytes 786436
  5.3 55.2 %all-to-all-start = ((f32[32,16,8,128]{3,2,1,0:T(8,128)}), f32[32,16,8,128]{3,2,1,0:T(8,128)S(1)}, u32[]{:S(2)}, u32[]{:S(2)}) async-start(f32[32,16,8,128]{3,2,1,0:T(8,128)} %bitcast.18), calls=%async_computation | async-start | bytes 4194304 | tf_op jit(solution)/shard_map/all_to_all | solution.py:870
  14.3 0.7 copy-start.6
  15.0 0.7 copy-start.7
  15.8 9.0 %collective-permute-start = (f32[160,512]{1,0:T(8,128)}, f32[160,512]{1,0:T(8,128)S(1)}, u32[]{:S(2)}, u32[]{:S(2)}) collective-permute-start(f32[160,512]{1,0:T(8,128)} %get-tuple-element.46), channel_id=1, source_target_pairs={{0,2},{2,0},{4,6},{6,4},{8,10},{10,8},{12,14},{14,12},{1,3},{3,1},... | collective-permute-start | bytes 983048 | tf_op jit(solution)/shard_map/ppermute | solution.py:808
  16.0 4.8 %collective-permute-start.1 = (f32[16,512]{1,0:T(8,128)S(1)}, f32[16,512]{1,0:T(8,128)S(1)}, u32[]{:S(2)}, u32[]{:S(2)}) collective-permute-start(f32[16,512]{1,0:T(8,128)S(1)} %get-tuple-element.47), channel_id=1, source_target_pairs={{0,1},{1,16},{16,17},{2,3},{3,18},{18,19},{4,5},{5,20},{20,21},{6,... | collective-permute-start | bytes 98312 | tf_op jit(solution)/shard_map/ppermute | solution.py:802
  19.4 5.3 %collective-permute-start.2 = (f32[16,512]{1,0:T(8,128)S(1)}, f32[16,512]{1,0:T(8,128)S(1)}, u32[]{:S(2)}, u32[]{:S(2)}) collective-permute-start(f32[16,512]{1,0:T(8,128)S(1)} %get-tuple-element.48), channel_id=1, source_target_pairs={{1,0},{16,1},{17,16},{3,2},{18,3},{19,18},{5,4},{20,5},{21,20},{7,... | collective-permute-start | bytes 98312 | tf_op jit(solution)/shard_map/ppermute | solution.py:802
  20.8 51.0 %copy-start.10 = (f32[16,512]{1,0:T(8,128)}, f32[16,512]{1,0:T(8,128)S(1)}, u32[]{:S(2)}) copy-start(f32[16,512]{1,0:T(8,128)S(1)} %collective-permute-done.1.rest_4_) | copy-start | bytes 98308
  24.7 47.1 %copy-start.11 = (f32[16,512]{1,0:T(8,128)}, f32[16,512]{1,0:T(8,128)S(1)}, u32[]{:S(2)}) copy-start(f32[16,512]{1,0:T(8,128)S(1)} %collective-permute-done.2.rest_5_) | copy-start | bytes 98308
  24.7 47.1 %copy-start.8 = (f32[160,512]{1,0:T(8,128)}, f32[160,512]{1,0:T(8,128)S(1)}, u32[]{:S(2)}) copy-start(f32[160,512]{1,0:T(8,128)S(1)} %collective-permute-done.rest_3_) | copy-start | bytes 983044
  60.5 11.4 %collective-permute-start.3 = (f32[160,512]{1,0:T(8,128)}, f32[160,512]{1,0:T(8,128)S(1)}, u32[]{:S(2)}, u32[]{:S(2)}) collective-permute-start(f32[160,512]{1,0:T(8,128)} %copy-done.7), channel_id=1, source_target_pairs={{2,4},{4,2},{6,8},{8,6},{10,12},{12,10},{3,5},{5,3},{7,9},{9,7},{1... | collective-permute-start | bytes 983048 | tf_op jit(solution)/shard_map/ppermute | solution.py:808
  71.9 0.7 copy-start.9
  72.6 59.1 %all-to-all-start.1 = ((f32[32,19,8,128]{3,2,1,0:T(8,128)}), f32[32,19,8,128]{3,2,1,0:T(8,128)S(1)}, u32[]{:S(2)}, u32[]{:S(2)}) async-start(f32[32,19,8,128]{3,2,1,0:T(8,128)} %shard_map.214), calls=%async_computation.1 | async-start | bytes 4980736 | tf_op jit(solution)/shard_map/all_to_all | solution.py:935
  77.5 1.2 copy-start.1
  78.7 1.0 copy-start.3
  131.8 7.3 %copy-start.2 = (f32[6,4,144,128]{3,2,1,0:T(8,128)S(1)}, f32[6,4,144,128]{3,2,1,0:T(8,128)}, u32[]{:S(2)}) copy-start(f32[6,4,144,128]{3,2,1,0:T(8,128)} %copy-done.1) | copy-start | bytes 5308420
  135.4 12.0 %collective-permute-start.4 = (f32[1296,128]{1,0:T(8,128)S(1)}, f32[1296,128]{1,0:T(8,128)S(1)}, u32[]{:S(2)}, u32[]{:S(2)}) collective-permute-start(f32[1296,128]{1,0:T(8,128)S(1)} %get-tuple-element.81), channel_id=1, source_target_pairs={{2,4},{4,2},{6,8},{8,6},{10,12},{12,10},{3,5},{5,3},{7,9},{9,7},{1... | collective-permute-start | bytes 1990664 | tf_op jit(solution)/shard_map/ppermute | solution.py:808
  139.0 8.5 %collective-permute-start.5 = (f32[1296,128]{1,0:T(8,128)S(1)}, f32[1296,128]{1,0:T(8,128)S(1)}, u32[]{:S(2)}, u32[]{:S(2)}) collective-permute-start(f32[1296,128]{1,0:T(8,128)S(1)} %get-tuple-element.82), channel_id=1, source_target_pairs={{0,2},{2,0},{4,6},{6,4},{8,10},{10,8},{12,14},{14,12},{1,3},{3,1},... | collective-permute-start | bytes 1990664 | tf_op jit(solution)/shard_map/ppermute | solution.py:808
  139.1 8.4 %copy-start.4 = (f32[2,2,4,144,128]{4,3,2,1,0:T(8,128)S(1)}, f32[2,2,4,144,128]{4,3,2,1,0:T(8,128)}, u32[]{:S(2)}) copy-start(f32[2,2,4,144,128]{4,3,2,1,0:T(8,128)} %copy-done.3) | copy-start | bytes 3538948

commit v2 on v0

--- a/solution.py
+++ b/solution.py
@@ -377,7 +377,7 @@
         put_rows(ks, to + n, SUB, value[n * cells : (n + 1) * cells])
 
 
-def edge_kernel(sizes, flags, b, *rest):
+def edge_kernel(sizes, flags, b, f, cf, *rest):
     (devices, q_count, low, tiles, planes, length) = sizes
     away, (ks, cks, cols, far, near_edge), rest = rest[:7], rest[7:12], rest[12:]
     near, (lh, ll, mh, ml, sems) = rest[:7], rest[7:]
@@ -456,9 +456,9 @@
     odd_row = flags[4] == 1
     low_end = (jnp.where(odd_row, 2, 1), jnp.where(odd_row, 3, 0))
     high_end = (jnp.where(odd_row, 1, 2), jnp.where(odd_row, 0, 3))
-    for edge, of in ((far, low_end), (near_edge, high_end)):
+    for edge, of, group in ((far, low_end, flags[4]), (near_edge, high_end, 1 - flags[4])):
         at = 0
-        for held in (ks, cks):
+        for held, source in ((ks, f), (cks, cf)):
             count, end = held.shape[1], held.shape[2] - SUB
             for n in of:
                 for x in range(count):
@@ -468,16 +468,19 @@
                 edge[at + x : at + x + 1, :] = held[of[1], x, SUB - 1 : SUB, :]
                 edge[at + count + x : at + count + x + 1, :] = held[of[1], x, end : end + 1, :]
             at += SUB
+            for x in range(count):
+                edge[at : at + end - SUB, :] = source[group, x, SUB:end, :]
+                at += end - SUB
 
 
 def halo_row(h, cells):
     return SUB - 2 + h if h < 2 else SUB + cells + h - 2
 
 
-def source_kernel(planes, pairs, x, out, lo, hi, left, right, held, summed):
+def source_kernel(planes, pairs, x, out, left, right, held, summed):
     cells = x.shape[0] // planes
     length = x.shape[1]
-    half, fourth = cells // 2, cells // 4
+    half = cells // 2
     held[...] = dot(x[...], pairs[...])
     for n in range(planes // 2):
         top = 2 * n * cells
@@ -487,11 +490,6 @@
             out[n * half : (n + 1) * half, lanes] = (
                 summed[pl.ds(0, half, stride=2), :] + summed[pl.ds(1, half, stride=2), :]
             )
-    for edge, plane in ((lo, 0), (hi, planes - 1)):
-        edge[:cells, :] = x[plane * cells : (plane + 1) * cells, :].astype(jnp.float32)
-        at = plane // 2 * half
-        edge[cells:, : length // 2] = out[at : at + fourth, :]
-        edge[cells:, length // 2 :] = out[at + fourth : at + half, :]
     for edge, row in ((left, 0), (right, cells - 1)):
         edge[...] = jnp.zeros_like(edge)
         for n in range(planes):
@@ -575,21 +573,11 @@
             ]
 
 
-def put_block(fine, held, to, source, row, cells, length):
-    if fine:
-        put_rows(held, to, SUB, source[row : row + cells, :])
-    else:
-        half = cells // 2
-        put_rows(held, to, SUB, source[row : row + half, :length])
-        put_rows(held, to, SUB + half, source[row : row + half, length:])
-
-
 def layout_kernel(sizes, *rest):
-    away, outs, near, sems = rest[:6], rest[6:10], rest[10:16], rest[16]
+    away, outs, near, sems = rest[:4], rest[4:8], rest[8:12], rest[12]
     for copy in load(list(zip(away, near)), sems):
         copy.wait()
-    source, coarse_source, *edges = near
-    sides = edges[2:]
+    source, coarse_source, *sides = near
     for fine, inner, outer in ((True, *outs[:2]), (False, *outs[2:])):
         planes, cells, length = sizes if fine else [n // 2 for n in sizes]
         f = source if fine else coarse_source
@@ -604,9 +592,7 @@
         for p in range(1, planes - 1):
             plane(inner, p - 1, p)
         for group, p in enumerate((0, planes - 1)):
-            row = 0 if fine else 2 * cells
-            put_block(fine, outer.at[group], 0, edges[group], row, cells, length)
-            plane(outer.at[group], 1, p)
+            plane(outer, group, p)
 
 
 def inner_level(sizes, ks, fs, us, ws, rs):
@@ -660,90 +646,76 @@
         copy.wait()
 
 
-def outer_kernel(sizes, flags, *rest):
-    kept, coarse_kept, (k_far, k_near, _, out, coarse_out), rest = (
-        rest[:5],
-        rest[5:10],
-        rest[10:15],
-        rest[15:],
-    )
-    scratch = (rest[:6], rest[6:])
-    levels = (sizes, tuple(n // 2 for n in sizes))
-    start = 0
-    sent = []
-    for size, held, given, target in zip(
-        levels, scratch, (kept, coarse_kept), (out, coarse_out)
+def outer_kernel(sizes, near, flags, *rest):
+    aliased = 1 if near else 2
+    kept, coarse_kept, edge = rest[:5], rest[5:10], rest[10]
+    (out, coarse_out), scratch = rest[11 + aliased : 13 + aliased], rest[13 + aliased :]
+    half = len(scratch) // 2
+    group = 1 - flags[4] if near else flags[4]
+    inwards = lambda i, count: jnp.where(group == 0, i, count - 1 - i)
+    start, sent = 0, []
+    for size, held, given, target in (
+        (sizes, scratch[:half], kept, out),
+        ([n // 2 for n in sizes], scratch[half:], coarse_kept, coarse_out),
     ):
-        planes = size[0]
+        planes, rows, _ = size
         ks, fs, inner_us, inner_ws, inner_rs = given
-        halo, us, ws, rs, done, sems = held
+        halo, halo_f, us, ws, rs, done, sems = held
         tiles, ext = ks.shape[1:3]
-        rows = size[1]
-        for group, edge in ((flags[4], k_far), (1 - flags[4], k_near)):
-            at = start
-            for place in range(2 * tiles):
-                to = place * ext + SUB
-                halo[group, to : to + rows, :] = edge[at : at + rows, :]
-                at += rows
+        at = start
+        for place in range(2 * tiles):
+            to = place * ext + SUB
+            halo[to : to + rows, :] = edge[at : at + rows, :]
+            at += rows
+        for x in range(tiles):
+            to = (tiles + x) * ext
+            halo[to + SUB - 1 : to + SUB, :] = edge[at + x : at + x + 1, :]
+            to += SUB + rows
+            halo[to : to + 1, :] = edge[at + tiles + x : at + tiles + x + 1, :]
+        at += SUB
+        for x in range(tiles):
+            halo_f[0, x, SUB : SUB + rows, :] = edge[at : at + rows, :]
+            at += rows
+        start = at
+
+        @pl.when(flags[group] == 1)
+        def _():
             for x in range(tiles):
-                to = (tiles + x) * ext
-                halo[group, to + SUB - 1 : to + SUB, :] = edge[at + x : at + x + 1, :]
-                to += SUB + rows
-                halo[group, to : to + 1, :] = edge[at + tiles + x : at + tiles + x + 1, :]
-        start = at + SUB
-        for group in range(2):
-
-            @pl.when(flags[group] == 1)
-            def _():
-                for x in range(tiles):
-                    at = (tiles + x) * ext
-                    halo[group, at : at + ext, :] = ks[3 * group, x]
-
-        def both_ends(group, carry):
-            def halo_plane(slot):
-                def get(x, top, end):
-                    at = (slot * tiles + x) * ext
-                    return halo[group, at + top : at + end, :]
-
-                return get
-
-            inwards = lambda i, count: jnp.where(group == 0, i, count - 1 - i)
-            own = [plane_of(ks, inwards(i, 4)) for i in range(2)]
-            u, w = (
-                [plane_of(new, group, i) for i in range(2)]
-                + [plane_of(old, inwards(i, planes - 2)) for i in range(2)]
-                for new, old in ((us, inner_us), (ws, inner_ws))
-            )
-            around = ((halo_plane(1), halo_plane(0), own[0]), (own[0], halo_plane(1), own[1]))
-            for i, near in enumerate(around):
-
-                def store(x, top, end, u, w, r):
-                    at = (group, i, x, slice(top, end))
-                    us[at], ws[at] = u, w
-                    if i == 1:
-                        rs[group, x, top:end, :] = r
-
-                first_sweep(tiles, ext, *near, plane_of(fs, group, i), store)
-            scales = (plane_of(rs, group), plane_of(inner_rs, inwards(0, planes - 2)))
-            for i, r in enumerate(scales):
-
-                def store(x, top, end, value):
-                    done[group, i, top - SUB : end - SUB, x * LANE : (x + 1) * LANE] = value
-
-                second_sweep(tiles, ext, own[i], u[i : i + 3], w[i : i + 3], r, store)
-                pltpu.make_async_copy(
-                    done.at[group, i], target.at[inwards(i, planes)], sems.at[2 * group + i]
-                ).start()
-            return carry
-
-        lax.fori_loop(0, 2, both_ends, 0)
-        for group, at in enumerate(((0, 1), (planes - 1, planes - 2))):
-            for i, p in enumerate(at):
-                sent.append(
-                    pltpu.make_async_copy(
-                        done.at[group, i], target.at[p], sems.at[2 * group + i]
-                    )
-                )
+                at = (tiles + x) * ext
+                halo[at : at + ext, :] = ks[3 * group, x]
+
+        def halo_plane(slot):
+            def get(x, top, end):
+                at = (slot * tiles + x) * ext
+                return halo[at + top : at + end, :]
+
+            return get
+
+        own = [plane_of(ks, inwards(i, 4)) for i in range(2)]
+        u, w = (
+            [plane_of(new, i) for i in range(2)]
+            + [plane_of(old, inwards(i, planes - 2)) for i in range(2)]
+            for new, old in ((us, inner_us), (ws, inner_ws))
+        )
+        around = ((halo_plane(1), halo_plane(0), own[0]), (own[0], halo_plane(1), own[1]))
+        sources = (plane_of(halo_f, 0), plane_of(fs, group))
+        for i in range(2):
+
+            def store(x, top, end, u, w, r):
+                at = (i, x, slice(top, end))
+                us[at], ws[at] = u, w
+                if i == 1:
+                    rs[0, x, top:end, :] = r
+
+            first_sweep(tiles, ext, *around[i], sources[i], store)
+        scales = (plane_of(rs, 0), plane_of(inner_rs, inwards(0, planes - 2)))
+        for i, r in enumerate(scales):
+
+            def store(x, top, end, value):
+                done[i, top - SUB : end - SUB, x * LANE : (x + 1) * LANE] = value
+
+            second_sweep(tiles, ext, own[i], u[i : i + 3], w[i : i + 3], r, store)
+            sent += send([(done.at[i], target.at[inwards(i, planes)])], sems, i)
     for copy in sent:
         copy.wait()
 
@@ -803,12 +775,13 @@
 def outer_scratch(size):
     planes, cells, length = size
     return room(
-        f32(2, 2 * (length // LANE) * (cells + 2 * SUB), LANE),
-        held_planes(size, 2, 2),
-        held_planes(size, 2, 2),
+        f32(2 * (length // LANE) * (cells + 2 * SUB), LANE),
+        held_planes(size, 1),
         held_planes(size, 2),
-        f32(2, 2, cells, length),
-    ) + [pltpu.SemaphoreType.DMA((4,))]
+        held_planes(size, 2),
+        held_planes(size, 1),
+        f32(2, cells, length),
+    ) + [pltpu.SemaphoreType.DMA((2,))]
 
 
 def fused_body(noise, source):
@@ -858,11 +831,10 @@
 
     pairs = np.zeros((length, length // 2), np.float32)
     pairs[np.arange(length), np.arange(length) // 2] = 0.125
-    level = f32(cells + cells // 4, length)
     side = f32(2 * SUB, length)
-    coarse_source, *edges = call(
+    coarse_source, *sides = call(
         functools.partial(source_kernel, planes),
-        [f32(planes * cells // 4, length // 2), level, level, side, side],
+        [f32(planes * cells // 4, length // 2), side, side],
         (pairs.astype(bf16), source.reshape(flat)),
         [
             pltpu.VMEM((planes * cells, length // 2), jnp.float32),
@@ -873,8 +845,8 @@
         12,
     )
     coarse_source = coarse_source.reshape(planes // 2, cells // 2, length // 2)
-    edges = (*swap(*edges[:2], "row"), *swap(*edges[2:], PLANE))
-    arrived, edges, coarse_source = lax.optimization_barrier((arrived, edges, coarse_source))
+    sides = swap(*sides, PLANE)
+    arrived, sides, coarse_source = lax.optimization_barrier((arrived, sides, coarse_source))
 
     constants = (
         two_parts(second_table(second))
@@ -912,24 +884,24 @@
         [SMEM, VMEM] + [AWAY] * len(constants),
         22,
     )
-    out, source, coarse_source, edges = lax.optimization_barrier(
-        (out, source, coarse_source, edges)
+    out, source, coarse_source, sides = lax.optimization_barrier(
+        (out, source, coarse_source, sides)
     )
     got = lax.all_to_all(out, EVERY, split_axis=0, concat_axis=0, tiled=True)
     size, coarse_size = noise.shape, coarse_source.shape
     sizes = (size, coarse_size)
-    sources = (source, coarse_source, *edges)
+    sources = (source, coarse_source, *sides)
     laid = call(
         functools.partial(layout_kernel, size),
         [
-            held_planes(s, *count)
+            held_planes(s, count)
             for s in sizes
-            for count in ((s[0] - 2,), (2, 2))
+            for count in (s[0] - 2, 2)
         ],
         sources,
-        room(*sources) + [pltpu.SemaphoreType.DMA((6,))],
+        room(*sources) + [pltpu.SemaphoreType.DMA((4,))],
         source.size,
-        [AWAY] * 6,
+        [AWAY] * 4,
         12,
     )
     got, laid = lax.optimization_barrier((got, laid))
@@ -941,19 +913,20 @@
         + (lane_order(2 * held, low).astype(bf16),)
         + two_parts(third_coarse_halo(length // 2, devices, js[:low]))
     )
-    edge = f32(sum(2 * (s[2] // LANE) * s[1] + SUB for s in sizes), LANE)
+    edge = f32(sum(3 * (s[2] // LANE) * s[1] + SUB for s in sizes), LANE)
     shares = (devices, 2 * held, tiles)
+    inner_f, outer_f, coarse_inner_f, coarse_outer_f = laid
     got = got.reshape(devices * tiles * SUB, LANE)
     ks, coarse_ks, cols, far, near = call(
         functools.partial(edge_kernel, (devices, 2 * held, low, tiles, planes, length)),
         [held_planes(s, 4) for s in sizes] + [f32(HALO * planes, length), edge, edge],
-        (flags, got, *constants),
+        (flags, got, outer_f, coarse_outer_f, *constants),
         room(*constants)
         + [pltpu.VMEM((2, 4 * cells, devices * held), bf16)] * 2
         + [pltpu.VMEM((planes // 2 * LANE, devices * low), bf16)] * 2
         + [pltpu.SemaphoreType.DMA((7,))],
         3 * planes * cells * length * length,
-        [SMEM, VMEM] + [AWAY] * 7,
+        [SMEM] + [VMEM] * 3 + [AWAY] * 7,
         16,
     )
     k_far, k_near = (
@@ -962,7 +935,6 @@
         )
         for x, at in ((far, 1), (near, 0))
     )
-    inner_f, outer_f, coarse_inner_f, coarse_outer_f = laid
     inner, *kept = call(
         functools.partial(inner_kernel, size, shares),
         [pltpu.HBM(size, jnp.float32)] + [held_planes(s, s[0] - 2) for s in sizes for _ in range(3)],
@@ -975,17 +947,21 @@
         [SMEM, VMEM] + [AWAY] * 2 + [VMEM] * 5,
         18,
     )
-    return call(
-        functools.partial(outer_kernel, size),
-        [pltpu.HBM(s, jnp.float32) for s in sizes],
-        (flags, ks, outer_f, *kept[:3], coarse_ks, coarse_outer_f, *kept[3:], k_far, k_near, inner),
-        outer_scratch(size) + outer_scratch(coarse_size),
-        30 * source.size,
-        [SMEM] + [VMEM] * 12 + [AWAY],
-        18,
-        None,
-        {13: 0},
-    )
+    own = (flags, ks, outer_f, *kept[:3], coarse_ks, coarse_outer_f, *kept[3:])
+    done = (inner,)
+    for near, edge in ((True, k_near), (False, k_far)):
+        done = call(
+            functools.partial(outer_kernel, size, near),
+            [pltpu.HBM(s, jnp.float32) for s in sizes],
+            (*own, edge, *done),
+            outer_scratch(size) + outer_scratch(coarse_size),
+            15 * source.size,
+            [SMEM] + [VMEM] * 11 + [AWAY] * len(done),
+            14,
+            None,
+            {12 + i: i for i in range(len(done))},
+        )
+    return tuple(done)
 
 
 NEIGHBOUR_STEPS = ((1, 0, 0), (-1, 0, 0), (0, 1, 0), (0, -1, 0), (0, 0, 1), (0, 0, -1))

time: 151 us -> 152 us (level)
  waiting for transfers between devices: 90.7 us -> 99.7 us
  starting transfers between devices: 27.4 us -> 19.6 us
    all_to_all x1, waiting for transfers between devices: 9.98 us -> 36.4 us  [fused_body(): lax.all_to_all(sent, EVERY, split_axis=0, concat_axis=0, tiled=True)]
    ppermute x4 -> x2, waiting for transfers between devices: 26.1 us -> 5.75 us  [swap(): return (lax.ppermute(hi, axis, up), lax.ppermute(lo, axis, down))]
    ppermute x4 -> x2, starting transfers between devices: 9.83 us -> 4.57 us  [swap(): return (lax.ppermute(hi, axis, up), lax.ppermute(lo, axis, down))]
    all_to_all x1, starting transfers between devices: 6.9 us -> 4.28 us  [fused_body(): got = lax.all_to_all(out, EVERY, split_axis=0, concat_axis=0, tiled=True)]
    ppermute x2, waiting for transfers between devices: 2.14 us -> 3.82 us  [fused_body(): lax.ppermute(x, 'row', [p for i in range(at, rows - 1, 2) for p in ((i, i...]
    pallas_call x7 -> x8, Pallas kernels: 28.8 us -> 29.3 us  [call(): pl.pallas_call(kernel, out_shape=outs, in_specs=specs, out_specs=out_spec...]
  transfers between devices with their start and end apart: 8 -> 6, of which waited for: 5 -> 5; matrix products, arithmetic and copies ran while one was open for 0% -> 0% of each run, Pallas kernels for 6% -> 7%
where the time goes in v2:
time: 152 us
  waiting for transfers between devices  99.7 us (66%)
  Pallas kernels  29.3 us (19%)
  starting transfers between devices  19.6 us (13%)
  local copies, waits for them, and re-layouts  2.11 us (1%)
    all_to_all x1, waiting for transfers between devices, fused_body(): got = lax.all_to_all(out, EVERY, split_axis=0, concat_axis=0, tiled=True)  53.7 us
    all_to_all x1, waiting for transfers between devices, fused_body(): lax.all_to_all(sent, EVERY, split_axis=0, concat_axis=0, tiled=True)  36.4 us
    pallas_call x8, Pallas kernels, call(): pl.pallas_call(kernel, out_shape=outs, in_specs=specs, out_specs=out_spec...  29.3 us
    all_to_all x1, starting transfers between devices, fused_body(): lax.all_to_all(sent, EVERY, split_axis=0, concat_axis=0, tiled=True)  7.1 us
    ppermute x2, waiting for transfers between devices, swap(): return (lax.ppermute(hi, axis, up), lax.ppermute(lo, axis, down))  5.75 us
    ppermute x2, starting transfers between devices, swap(): return (lax.ppermute(hi, axis, up), lax.ppermute(lo, axis, down))  4.57 us
    all_to_all x1, starting transfers between devices, fused_body(): got = lax.all_to_all(out, EVERY, split_axis=0, concat_axis=0, tiled=True)  4.28 us
    ppermute x2, waiting for transfers between devices, fused_body(): lax.ppermute(x, 'row', [p for i in range(at, rows - 1, 2) for p in ((i, i...  3.82 us
  transfers between devices with their start and end apart: 6, of which 5 were waited for; matrix products, arithmetic and copies ran while one was open for 0% of the time, Pallas kernels for 7%

profile of v2, /device:TPU:1, one launch (start us, length us, event | category | flops | bytes accessed | tf_op | source)
XLA Modules:
  0.0 151.6 jit_solution(7863471450092596386)
XLA Ops:
  0.6 4.6 %shard_map.212 = f32[4096,128]{1,0:T(8,128)} custom-call(bf16[4,256,512]{2,1,0:T(8,128)(2,1)} %constant.80.clone.d_hbm, bf16[1024,512]{1,0:T(8,128)(2,1)} %bitcast.19), custom_call_target="tpu_custom_call" | custom-call | flops 1073741824 | bytes 4194304 | tf_op jit(solution)/shard_map/pallas_call | solution.py:740
  5.3 0.0 copy-start.3
  5.3 7.1 %all-to-all-start = ((f32[32,16,8,128]{3,2,1,0:T(8,128)}), f32[32,16,8,128]{3,2,1,0:T(8,128)S(1)}, u32[]{:S(2)}, u32[]{:S(2)}) async-start(f32[32,16,8,128]{3,2,1,0:T(8,128)} %bitcast.18), calls=%async_computation | async-start | bytes 4194304 | tf_op jit(solution)/shard_map/all_to_all | solution.py:830
  12.4 0.5 shard_map.213
  12.9 0.7 copy-done.4
  13.6 3.3 %collective-permute-start = (f32[16,512]{1,0:T(8,128)S(1)}, f32[16,512]{1,0:T(8,128)S(1)}, u32[]{:S(2)}, u32[]{:S(2)}) collective-permute-start(f32[16,512]{1,0:T(8,128)S(1)} %get-tuple-element.41), channel_id=1, source_target_pairs={{0,1},{1,16},{16,17},{2,3},{3,18},{18,19},{4,5},{5,20},{20,21},{6,... | collective-permute-start | bytes 98312 | tf_op jit(solution)/shard_map/ppermute | solution.py:767
  16.9 1.3 collective-permute-start.1
  18.2 0.1 copy.28.scale
  18.3 1.4 collective-permute-done.rest_2_
  19.7 4.4 %collective-permute-done.1.rest_3_ = f32[16,512]{1,0:T(8,128)S(1)} collective-permute-done((f32[16,512]{1,0:T(8,128)S(1)}, f32[16,512]{1,0:T(8,128)S(1)}, u32[]{:S(2)}, u32[]{:S(2)}) %collective-permute-start.1) | collective-permute-done | bytes 32800 | tf_op jit(solution)/shard_map/ppermute | solution.py:767
  24.1 36.4 %all-to-all-done.b = f32[32,16,8,128]{3,2,1,0:T(8,128)S(1)} async-done(((f32[32,16,8,128]{3,2,1,0:T(8,128)}), f32[32,16,8,128]{3,2,1,0:T(8,128)S(1)}, u32[]{:S(2)}, u32[]{:S(2)}) %all-to-all-start) | async-done | bytes 2097184 | tf_op jit(solution)/shard_map/all_to_all | solution.py:830
  60.5 7.4 %shard_map.214 = f32[32,19,8,128]{3,2,1,0:T(8,128)} custom-call(f32[8,2]{1,0:T(8,128)S(1)} %copy.28.scale, f32[32,16,8,128]{3,2,1,0:T(8,128)S(1)} %all-to-all-done.b, bf16[2,256,256]{2,1,0:T(8,128)(2,1)} %constant.83.clone.rest_0_, bf16[2,256,256]{2,1,0:T(8,128)(2,1)} %constant.84.clone.rest_1_, bf16[256,256]{1,0:T(8,128)(2,1)} %constant.85.clone.rest_2_, ...), custom_call_target="tpu_custom_call" | custom-call | flops 4026531840 | bytes 7012416 | tf_op jit(solution)/shard_map/pallas_call | solution.py:740
  67.9 4.3 %all-to-all-start.1 = ((f32[32,19,8,128]{3,2,1,0:T(8,128)}), f32[32,19,8,128]{3,2,1,0:T(8,128)S(1)}, u32[]{:S(2)}, u32[]{:S(2)}) async-start(f32[32,19,8,128]{3,2,1,0:T(8,128)} %shard_map.214), calls=%async_computation.1 | async-start | bytes 4980736 | tf_op jit(solution)/shard_map/all_to_all | solution.py:890
  72.2 0.1 stack.32
  72.3 1.5 shard_map.215
  73.8 1.2 copy-done.1
  75.0 53.7 %all-to-all-done.1 = f32[32,19,8,128]{3,2,1,0:T(8,128)S(1)} async-done(((f32[32,19,8,128]{3,2,1,0:T(8,128)}), f32[32,19,8,128]{3,2,1,0:T(8,128)S(1)}, u32[]{:S(2)}, u32[]{:S(2)}) %all-to-all-start.1) | async-done | bytes 2490400 | tf_op jit(solution)/shard_map/all_to_all | solution.py:890
  128.7 3.7 %shard_map.216 = (f32[4,4,144,128]{3,2,1,0:T(8,128)S(1)}, f32[4,2,80,128]{3,2,1,0:T(8,128)S(1)}, f32[32,512]{1,0:T(8,128)S(1)}, f32[1936,128]{1,0:T(8,128)S(1)}, f32[1936,128]{1,0:T(8,128)S(1)}) custom-call(s32[5]{0:T(128)S(1)} %convert_element_type.6.flags, f32[4864,128]{1,0:T(8,128)S(1)} %bitcast.14, f32[2,4,144,128]{3,2,1,0:T(8,128)S(1)} %get-tuple-element.58.f.rest_1_, ...), custom_call_target="tpu_custom_call" | custom-call | flops 805306368 | bytes 7880724 | tf_op jit(solution)/shard_map/pallas_call | solution.py:740
  132.5 0.9 collective-permute-start.3
  133.4 2.7 %collective-permute-start.2 = (f32[1936,128]{1,0:T(8,128)S(1)}, f32[1936,128]{1,0:T(8,128)S(1)}, u32[]{:S(2)}, u32[]{:S(2)}) collective-permute-start(f32[1936,128]{1,0:T(8,128)S(1)} %get-tuple-element.71), channel_id=1, source_target_pairs={{2,4},{4,2},{6,8},{8,6},{10,12},{12,10},{3,5},{5,3},{7,9},{9,7},{1... | collective-permute-start | bytes 2973704 | tf_op jit(solution)/shard_map/ppermute | solution.py:933
  136.1 6.3 %shard_map.217 = (f32[8,128,512]{2,1,0:T(8,128)}, f32[6,4,144,128]{3,2,1,0:T(8,128)S(1)}, f32[6,4,144,128]{3,2,1,0:T(8,128)S(1)}, f32[6,4,144,128]{3,2,1,0:T(8,1...) custom-call(s32[5]{0:T(128)S(1)} %convert_element_type.6.flags, ...), custom_call_target="tpu_custom_call" | custom-call | flops 805306368 | bytes 14417940 | tf_op jit(solution)/shard_map/pallas_call | solution.py:740
  142.4 2.7 %shard_map.218 = (f32[8,128,512]{2,1,0:T(8,128)}, f32[4,64,256]{2,1,0:T(8,128)}) custom-call(s32[5]{0:T(128)S(1)} %convert_element_type.6.flags, f32[4,4,144,128]{3,2,1,0:T(8,128)S(1)} %get-tuple-element.60.edges.rest_0_, f32[2,4,144,128]{3,2,1,0:T(8,128)S(1)} %get-tuple-element.58.f.rest_1_, ...), custom_call_target="tpu_custom_call", output_to_operand_aliasing={{0}: (12, {})} | custom-call | flops 7864320 | bytes 13508628 | tf_op jit(solution)/shard_map/pallas_call | solution.py:740
  145.1 3.8 %collective-permute-done.2.rest_10_ = f32[1936,128]{1,0:T(8,128)S(1)} collective-permute-done((f32[1936,128]{1,0:T(8,128)S(1)}, f32[1936,128]{1,0:T(8,128)S(1)}, u32[]{:S(2)}, u32[]{:S(2)}) %collective-permute-start.2) | collective-permute-done | bytes 991264 | tf_op jit(solution)/shard_map/ppermute | solution.py:933
  148.9 2.7 %shard_map.219 = (f32[8,128,512]{2,1,0:T(8,128)}, f32[4,64,256]{2,1,0:T(8,128)}) custom-call(s32[5]{0:T(128)S(1)} %convert_element_type.6.flags, f32[4,4,144,128]{3,2,1,0:T(8,128)S(1)} %get-tuple-element.60.edges.rest_0_, f32[2,4,144,128]{3,2,1,0:T(8,128)S(1)} %get-tuple-element.58.f.rest_1_, ...), custom_call_target="tpu_custom_call", output_to_operand_aliasing={{0}: (12, {}), {1}: (13, {})} | custom-call | flops 7864320 | bytes 13770772 | tf_op jit(solution)/shard_map/pallas_call | solution.py:740
  (15 shorter events, 0.1 us)
Async XLA Ops:
  5.3 7.1 %copy-start = (bf16[8,128,512]{2,1,0:T(8,128)(2,1)S(1)}, bf16[8,128,512]{2,1,0:T(8,128)(2,1)}, u32[]{:S(2)}) copy-start(bf16[8,128,512]{2,1,0:T(8,128)(2,1)} %rest_0_.2) | copy-start | bytes 3145732
  5.3 7.1 %copy-start.3 = (bf16[512,256]{1,0:T(8,128)(2,1)S(1)}, bf16[512,256]{1,0:T(8,128)(2,1)}, u32[]{:S(2)}) copy-start(bf16[512,256]{1,0:T(8,128)(2,1)} %constant.81.clone.pairs) | copy-start | bytes 786436
  5.3 55.2 %all-to-all-start = ((f32[32,16,8,128]{3,2,1,0:T(8,128)}), f32[32,16,8,128]{3,2,1,0:T(8,128)S(1)}, u32[]{:S(2)}, u32[]{:S(2)}) async-start(f32[32,16,8,128]{3,2,1,0:T(8,128)} %bitcast.18), calls=%async_computation | async-start | bytes 4194304 | tf_op jit(solution)/shard_map/all_to_all | solution.py:830
  12.9 0.7 copy-start.4
  13.6 6.1 %collective-permute-start = (f32[16,512]{1,0:T(8,128)S(1)}, f32[16,512]{1,0:T(8,128)S(1)}, u32[]{:S(2)}, u32[]{:S(2)}) collective-permute-start(f32[16,512]{1,0:T(8,128)S(1)} %get-tuple-element.41), channel_id=1, source_target_pairs={{0,1},{1,16},{16,17},{2,3},{3,18},{18,19},{4,5},{5,20},{20,21},{6,... | collective-permute-start | bytes 98312 | tf_op jit(solution)/shard_map/ppermute | solution.py:767
  16.9 7.2 %collective-permute-start.1 = (f32[16,512]{1,0:T(8,128)S(1)}, f32[16,512]{1,0:T(8,128)S(1)}, u32[]{:S(2)}, u32[]{:S(2)}) collective-permute-start(f32[16,512]{1,0:T(8,128)S(1)} %get-tuple-element.42), channel_id=1, source_target_pairs={{1,0},{16,1},{17,16},{3,2},{18,3},{19,18},{5,4},{20,5},{21,20},{7,... | collective-permute-start | bytes 98312 | tf_op jit(solution)/shard_map/ppermute | solution.py:767
  19.7 48.2 %copy-start.5 = (f32[16,512]{1,0:T(8,128)}, f32[16,512]{1,0:T(8,128)S(1)}, u32[]{:S(2)}) copy-start(f32[16,512]{1,0:T(8,128)S(1)} %collective-permute-done.rest_2_) | copy-start | bytes 98308
  24.1 43.8 %copy-start.6 = (f32[16,512]{1,0:T(8,128)}, f32[16,512]{1,0:T(8,128)S(1)}, u32[]{:S(2)}) copy-start(f32[16,512]{1,0:T(8,128)S(1)} %collective-permute-done.1.rest_3_) | copy-start | bytes 98308
  67.9 60.9 %all-to-all-start.1 = ((f32[32,19,8,128]{3,2,1,0:T(8,128)}), f32[32,19,8,128]{3,2,1,0:T(8,128)S(1)}, u32[]{:S(2)}, u32[]{:S(2)}) async-start(f32[32,19,8,128]{3,2,1,0:T(8,128)} %shard_map.214), calls=%async_computation.1 | async-start | bytes 4980736 | tf_op jit(solution)/shard_map/all_to_all | solution.py:890
  73.8 1.2 copy-start.1
  128.7 7.4 %copy-start.2 = (f32[6,4,144,128]{3,2,1,0:T(8,128)S(1)}, f32[6,4,144,128]{3,2,1,0:T(8,128)}, u32[]{:S(2)}) copy-start(f32[6,4,144,128]{3,2,1,0:T(8,128)} %copy-done.1) | copy-start | bytes 5308420
  132.5 9.9 %collective-permute-start.3 = (f32[1936,128]{1,0:T(8,128)S(1)}, f32[1936,128]{1,0:T(8,128)S(1)}, u32[]{:S(2)}, u32[]{:S(2)}) collective-permute-start(f32[1936,128]{1,0:T(8,128)S(1)} %get-tuple-element.72), channel_id=1, source_target_pairs={{0,2},{2,0},{4,6},{6,4},{8,10},{10,8},{12,14},{14,12},{1,3},{3,1},... | collective-permute-start | bytes 2973704 | tf_op jit(solution)/shard_map/ppermute | solution.py:933
  133.4 15.5 %collective-permute-start.2 = (f32[1936,128]{1,0:T(8,128)S(1)}, f32[1936,128]{1,0:T(8,128)S(1)}, u32[]{:S(2)}, u32[]{:S(2)}) collective-permute-start(f32[1936,128]{1,0:T(8,128)S(1)} %get-tuple-element.71), channel_id=1, source_target_pairs={{2,4},{4,2},{6,8},{8,6},{10,12},{12,10},{3,5},{5,3},{7,9},{9,7},{1... | collective-permute-start | bytes 2973704 | tf_op jit(solution)/shard_map/ppermute | solution.py:933

commit v3 on v0

--- a/solution.py
+++ b/solution.py
@@ -550,6 +550,17 @@
             store(x, top, end, value)
 
 
+def around(tiles, ext, mid, beyond, store):
+    for top in range(0, ext, SUB):
+        end = top + SUB
+        parts = [mid(x, top, end) for x in range(tiles)]
+        for x, both in enumerate(beside(parts, (parts[0], parts[-1]))):
+            k = parts[x]
+            above = pltpu.roll(k, 1, 0) if top == 0 else mid(x, top - 1, end - 1)
+            below = pltpu.roll(k, SUB - 1, 0) if end == ext else mid(x, top + 1, end + 1)
+            store(x, top, end, (6.0 * k + beyond(x, top, end)) + (above + below) + both)
+
+
 def plane_of(held, *at):
     return lambda x, top, end: held[(*at, x, slice(top, end), slice(None))]
 
@@ -625,8 +636,36 @@
     lax.fori_loop(1, planes - 1, first, 0)
 
 
+def prepare(ks, us, ws, rs, sums, ready):
+    planes, tiles, ext, _ = ks.shape
+
+    def end_of(group, carry):
+        inwards = lambda i, count: jnp.where(group == 0, i, count - 1 - i)
+
+        def store_sum(x, top, end, value):
+            sums[group, x, top:end, :] = value
+
+        own = [plane_of(ks, inwards(i, planes)) for i in range(2)]
+        around(tiles, ext, *own, store_sum)
+
+        def store(x, top, end, value):
+            ready[group, x, top:end, :] = value
+
+        nothing = lambda x, top, end: 0.0
+        u, w = (
+            [nothing] + [plane_of(held, inwards(i, planes - 2)) for i in range(2)]
+            for held in (us, ws)
+        )
+        scale = plane_of(rs, inwards(0, planes - 2))
+        second_sweep(tiles, ext, own[1], u, w, scale, store)
+        return carry
+
+    lax.fori_loop(0, 2, end_of, 0)
+
+
 def inner_kernel(sizes, shares, flags, b, eh_hbm, el_hbm, edges, cks, cols, fs, cfs, *rest):
-    out_hbm, us, ws, rs, cus, cws, crs, ks, eh, el, lh, ll, out, sems = rest
+    out_hbm, us, ws, rs, cus, cws, crs, sums, ready, csums, cready, *rest = rest
+    ks, eh, el, lh, ll, out, sems = rest
     planes, cells, length = sizes
     tiles, ext = ks.shape[1:3]
     copies = load([(eh_hbm, eh), (el_hbm, el)], sems)
@@ -655,17 +694,19 @@
 
     lax.fori_loop(2, planes - 2, second, 0)
     copies = send([(out, out_hbm.at[2 : planes - 2])], sems, 0)
+    prepare(ks, us, ws, rs, sums, ready)
     inner_level([n // 2 for n in sizes], cks, cfs, cus, cws, crs)
+    prepare(cks, cus, cws, crs, csums, cready)
     for copy in copies:
         copy.wait()
 
 
 def outer_kernel(sizes, flags, *rest):
     kept, coarse_kept, (k_far, k_near, _, out, coarse_out), rest = (
-        rest[:5],
-        rest[5:10],
-        rest[10:15],
-        rest[15:],
+        rest[:7],
+        rest[7:14],
+        rest[14:19],
+        rest[19:],
     )
     scratch = (rest[:6], rest[6:])
     levels = (sizes, tuple(n // 2 for n in sizes))
@@ -675,7 +716,7 @@
         levels, scratch, (kept, coarse_kept), (out, coarse_out)
     ):
         planes = size[0]
-        ks, fs, inner_us, inner_ws, inner_rs = given
+        ks, fs, inner_us, inner_ws, inner_rs, sums, ready = given
         halo, us, ws, rs, done, sems = held
         tiles, ext = ks.shape[1:3]
         rows = size[1]
@@ -709,28 +750,41 @@
 
             inwards = lambda i, count: jnp.where(group == 0, i, count - 1 - i)
             own = [plane_of(ks, inwards(i, 4)) for i in range(2)]
+            def store_outer(x, top, end, u, w, r):
+                at = (group, 0, x, slice(top, end))
+                us[at], ws[at] = u, w
+
+            beyond = halo_plane(1)
+            first_sweep(
+                tiles, ext, beyond, halo_plane(0), own[0], plane_of(fs, group, 0), store_outer
+            )
+            for top in range(0, ext, SUB):
+                for x in range(tiles):
+                    at = (x, slice(top, top + SUB))
+                    near_sum = sums[(group, *at)] + beyond(x, top, top + SUB)
+                    scale = JACOBI_WEIGHT / near_sum
+                    u = fs[(group, 1, *at)] * (2.0 * scale)
+                    us[(group, 1, *at)] = u
+                    ws[(group, 1, *at)] = own[0](x, top, top + SUB) * u
+                    rs[(group, *at)] = scale
             u, w = (
                 [plane_of(new, group, i) for i in range(2)]
-                + [plane_of(old, inwards(i, planes - 2)) for i in range(2)]
+                + [plane_of(old, inwards(0, planes - 2))]
                 for new, old in ((us, inner_us), (ws, inner_ws))
             )
-            around = ((halo_plane(1), halo_plane(0), own[0]), (own[0], halo_plane(1), own[1]))
-            for i, near in enumerate(around):
-
-                def store(x, top, end, u, w, r):
-                    at = (group, i, x, slice(top, end))
-                    us[at], ws[at] = u, w
-                    if i == 1:
-                        rs[group, x, top:end, :] = r
-
-                first_sweep(tiles, ext, *near, plane_of(fs, group, i), store)
-            scales = (plane_of(rs, group), plane_of(inner_rs, inwards(0, planes - 2)))
-            for i, r in enumerate(scales):
-
-                def store(x, top, end, value):
-                    done[group, i, top - SUB : end - SUB, x * LANE : (x + 1) * LANE] = value
-
-                second_sweep(tiles, ext, own[i], u[i : i + 3], w[i : i + 3], r, store)
+
+            def store(x, top, end, value):
+                done[group, 0, top - SUB : end - SUB, x * LANE : (x + 1) * LANE] = value
+
+            second_sweep(tiles, ext, own[0], u, w, plane_of(rs, group), store)
+            scale = plane_of(inner_rs, inwards(0, planes - 2))
+            for top in range(SUB, ext - SUB, SUB):
+                for x in range(tiles):
+                    at = (x, top, top + SUB)
+                    coupled = own[1](*at) * u[1](*at) + w[1](*at)
+                    value = ready[group, x, top : top + SUB, :] + scale(*at) * coupled
+                    done[group, 1, top - SUB : top, x * LANE : (x + 1) * LANE] = value
+            for i in range(2):
                 pltpu.make_async_copy(
                     done.at[group, i], target.at[inwards(i, planes)], sems.at[2 * group + i]
                 ).start()
@@ -965,7 +1019,9 @@
     inner_f, outer_f, coarse_inner_f, coarse_outer_f = laid
     inner, *kept = call(
         functools.partial(inner_kernel, size, shares),
-        [pltpu.HBM(size, jnp.float32)] + [held_planes(s, s[0] - 2) for s in sizes for _ in range(3)],
+        [pltpu.HBM(size, jnp.float32)]
+        + [held_planes(s, s[0] - 2) for s in sizes for _ in range(3)]
+        + [held_planes(s, 2) for s in sizes for _ in range(2)],
         (flags, got, *constants[:2], ks, coarse_ks, cols, inner_f, coarse_inner_f),
         room(held_planes(size, planes), *constants[:2])
         + [pltpu.VMEM((2, (planes - 4) * cells, devices * held), bf16)] * 2
@@ -978,13 +1034,18 @@
     return call(
         functools.partial(outer_kernel, size),
         [pltpu.HBM(s, jnp.float32) for s in sizes],
-        (flags, ks, outer_f, *kept[:3], coarse_ks, coarse_outer_f, *kept[3:], k_far, k_near, inner),
+        (
+            flags,
+            *(ks, outer_f, *kept[:3], *kept[6:8]),
+            *(coarse_ks, coarse_outer_f, *kept[3:6], *kept[8:]),
+            *(k_far, k_near, inner),
+        ),
         outer_scratch(size) + outer_scratch(coarse_size),
         30 * source.size,
-        [SMEM] + [VMEM] * 12 + [AWAY],
+        [SMEM] + [VMEM] * 16 + [AWAY],
         18,
         None,
-        {13: 0},
+        {17: 0},
     )
 
 

time: 151 us -> 150 us (level)
  transfers between devices with their start and end apart: 8 -> 8, of which waited for: 5 -> 5; matrix products, arithmetic and copies ran while one was open for 0% -> 0% of each run, Pallas kernels for 6% -> 7%
where the time goes in v3:
time: 150 us
  waiting for transfers between devices  90.1 us (60%)
  Pallas kernels  28.3 us (19%)
  starting transfers between devices  27.4 us (18%)
  local copies, waits for them, and re-layouts  3.15 us (2%)
    all_to_all x1, waiting for transfers between devices, fused_body(): got = lax.all_to_all(out, EVERY, split_axis=0, concat_axis=0, tiled=True)  52.5 us
    pallas_call x7, Pallas kernels, call(): pl.pallas_call(kernel, out_shape=outs, in_specs=specs, out_specs=out_spec...  28.3 us
    ppermute x4, waiting for transfers between devices, swap(): return (lax.ppermute(hi, axis, up), lax.ppermute(lo, axis, down))  26.1 us
    all_to_all x1, waiting for transfers between devices, fused_body(): lax.all_to_all(sent, EVERY, split_axis=0, concat_axis=0, tiled=True)  9.98 us
    ppermute x4, starting transfers between devices, swap(): return (lax.ppermute(hi, axis, up), lax.ppermute(lo, axis, down))  9.83 us
    all_to_all x1, starting transfers between devices, fused_body(): lax.all_to_all(sent, EVERY, split_axis=0, concat_axis=0, tiled=True)  7.1 us
    all_to_all x1, starting transfers between devices, fused_body(): got = lax.all_to_all(out, EVERY, split_axis=0, concat_axis=0, tiled=True)  6.9 us
    ppermute x2, starting transfers between devices, fused_body(): lax.ppermute(x, 'row', [p for i in range(at, rows - 1, 2) for p in ((i, i...  3.61 us
  transfers between devices with their start and end apart: 8, of which 5 were waited for; matrix products, arithmetic and copies ran while one was open for 0% of the time, Pallas kernels for 7%

profile of v3, /device:TPU:1, one launch (start us, length us, event | category | flops | bytes accessed | tf_op | source)
XLA Modules:
  0.0 149.9 jit_solution(1604966413735490735)
XLA Ops:
  0.6 4.6 %shard_map.212 = f32[4096,128]{1,0:T(8,128)} custom-call(bf16[4,256,512]{2,1,0:T(8,128)(2,1)} %constant.80.clone.d_hbm, bf16[1024,512]{1,0:T(8,128)(2,1)} %bitcast.19), custom_call_target="tpu_custom_call" | custom-call | flops 1073741824 | bytes 4194304 | tf_op jit(solution)/shard_map/pallas_call | solution.py:822
  5.3 7.1 %all-to-all-start = ((f32[32,16,8,128]{3,2,1,0:T(8,128)}), f32[32,16,8,128]{3,2,1,0:T(8,128)S(1)}, u32[]{:S(2)}, u32[]{:S(2)}) async-start(f32[32,16,8,128]{3,2,1,0:T(8,128)} %bitcast.18), calls=%async_computation | async-start | bytes 4194304 | tf_op jit(solution)/shard_map/all_to_all | solution.py:911
  12.4 1.3 shard_map.213
  13.7 0.7 copy-done.6
  14.4 3.5 %collective-permute-start = (f32[160,512]{1,0:T(8,128)}, f32[160,512]{1,0:T(8,128)S(1)}, u32[]{:S(2)}, u32[]{:S(2)}) collective-permute-start(f32[160,512]{1,0:T(8,128)} %get-tuple-element.49), channel_id=1, source_target_pairs={{0,2},{2,4},{4,6},{6,8},{8,10},{10,12},{12,14},{1,3},{3,5},{5,7},{... | collective-permute-start | bytes 983048 | tf_op jit(solution)/shard_map/ppermute | solution.py:849
  17.9 1.9 %collective-permute-start.1 = (f32[160,512]{1,0:T(8,128)}, f32[160,512]{1,0:T(8,128)S(1)}, u32[]{:S(2)}, u32[]{:S(2)}) collective-permute-start(f32[160,512]{1,0:T(8,128)} %get-tuple-element.50), channel_id=1, source_target_pairs={{2,0},{4,2},{6,4},{8,6},{10,8},{12,10},{14,12},{3,1},{5,3},{7,5},{... | collective-permute-start | bytes 983048 | tf_op jit(solution)/shard_map/ppermute | solution.py:849
  19.9 3.1 %collective-permute-start.2 = (f32[16,512]{1,0:T(8,128)S(1)}, f32[16,512]{1,0:T(8,128)S(1)}, u32[]{:S(2)}, u32[]{:S(2)}) collective-permute-start(f32[16,512]{1,0:T(8,128)S(1)} %get-tuple-element.51), channel_id=1, source_target_pairs={{0,1},{1,16},{16,17},{2,3},{3,18},{18,19},{4,5},{5,20},{20,21},{6,... | collective-permute-start | bytes 98312 | tf_op jit(solution)/shard_map/ppermute | solution.py:849
  23.0 1.3 collective-permute-start.3
  24.3 0.1 copy.26.scale
  24.4 4.0 %collective-permute-done.3.rest_5_ = f32[16,512]{1,0:T(8,128)S(1)} collective-permute-done((f32[16,512]{1,0:T(8,128)S(1)}, f32[16,512]{1,0:T(8,128)S(1)}, u32[]{:S(2)}, u32[]{:S(2)}) %collective-permute-start.3) | collective-permute-done | bytes 32800 | tf_op jit(solution)/shard_map/ppermute | solution.py:849
  28.4 22.1 %collective-permute-done.rest_2_ = f32[160,512]{1,0:T(8,128)S(1)} collective-permute-done((f32[160,512]{1,0:T(8,128)}, f32[160,512]{1,0:T(8,128)S(1)}, u32[]{:S(2)}, u32[]{:S(2)}) %collective-permute-start) | collective-permute-done | bytes 327712 | tf_op jit(solution)/shard_map/ppermute | solution.py:849
  50.5 10.0 %all-to-all-done.b = f32[32,16,8,128]{3,2,1,0:T(8,128)S(1)} async-done(((f32[32,16,8,128]{3,2,1,0:T(8,128)}), f32[32,16,8,128]{3,2,1,0:T(8,128)S(1)}, u32[]{:S(2)}, u32[]{:S(2)}) %all-to-all-start) | async-done | bytes 2097184 | tf_op jit(solution)/shard_map/all_to_all | solution.py:911
  60.5 7.3 %shard_map.214 = f32[32,19,8,128]{3,2,1,0:T(8,128)} custom-call(f32[8,2]{1,0:T(8,128)S(1)} %copy.26.scale, f32[32,16,8,128]{3,2,1,0:T(8,128)S(1)} %all-to-all-done.b, bf16[2,256,256]{2,1,0:T(8,128)(2,1)} %constant.83.clone.rest_0_, bf16[2,256,256]{2,1,0:T(8,128)(2,1)} %constant.84.clone.rest_1_, bf16[256,256]{1,0:T(8,128)(2,1)} %constant.85.clone.rest_2_, ...), custom_call_target="tpu_custom_call" | custom-call | flops 4026531840 | bytes 7012416 | tf_op jit(solution)/shard_map/pallas_call | solution.py:822
  67.9 6.9 %all-to-all-start.1 = ((f32[32,19,8,128]{3,2,1,0:T(8,128)}), f32[32,19,8,128]{3,2,1,0:T(8,128)S(1)}, u32[]{:S(2)}, u32[]{:S(2)}) async-start(f32[32,19,8,128]{3,2,1,0:T(8,128)} %shard_map.214), calls=%async_computation.1 | async-start | bytes 4980736 | tf_op jit(solution)/shard_map/all_to_all | solution.py:972
  74.8 0.1 stack.32
  74.9 1.7 %shard_map.215 = (f32[6,4,144,128]{3,2,1,0:T(8,128)S(1)}, f32[2,2,4,144,128]{4,3,2,1,0:T(8,128)S(1)}, f32[2,2,80,128]{3,2,1,0:T(8,128)S(1)}, f32[2,2,2,80,128]{4,3,2,1,0:T(8,128)S(1)}) custom-call(bf16[8,128,512]{2,1,0:T(8,128)(2,1)} %rest_0_.2, f32[4,64,256]{2,1,0:T(8,128)} %bitcast.17, f32[160,512]{1,0:T(8,128)} %copy-done.7, f32[160,512]{1,0:T(8,128)} %copy-done.8, ...), custom_call_target="tpu_custom_call" | custom-call | flops 524288 | bytes 5472256 | tf_op jit(solution)/shard_map/pallas_call | solution.py:822
  76.7 1.2 copy-done.1
  77.9 1.0 copy-done.3
  78.9 52.5 %all-to-all-done.1 = f32[32,19,8,128]{3,2,1,0:T(8,128)S(1)} async-done(((f32[32,19,8,128]{3,2,1,0:T(8,128)}), f32[32,19,8,128]{3,2,1,0:T(8,128)S(1)}, u32[]{:S(2)}, u32[]{:S(2)}) %all-to-all-start.1) | async-done | bytes 2490400 | tf_op jit(solution)/shard_map/all_to_all | solution.py:972
  131.4 3.7 %shard_map.216 = (f32[4,4,144,128]{3,2,1,0:T(8,128)S(1)}, f32[4,2,80,128]{3,2,1,0:T(8,128)S(1)}, f32[32,512]{1,0:T(8,128)S(1)}, f32[1296,128]{1,0:T(8,128)S(1)}, f32[1296,128]{1,0:T(8,128)S(1)}) custom-call(s32[5]{0:T(128)S(1)} %convert_element_type.6.flags, f32[4864,128]{1,0:T(8,128)S(1)} %bitcast.14, bf16[2,256,256]{2,1,0:T(8,128)(2,1)} %constant.92.clone.rest_0_.eh_hbm, ...), custom_call_target="tpu_custom_call" | custom-call | flops 805306368 | bytes 6471700 | tf_op jit(solution)/shard_map/pallas_call | solution.py:822
  135.1 3.5 %collective-permute-start.4 = (f32[1296,128]{1,0:T(8,128)S(1)}, f32[1296,128]{1,0:T(8,128)S(1)}, u32[]{:S(2)}, u32[]{:S(2)}) collective-permute-start(f32[1296,128]{1,0:T(8,128)S(1)} %get-tuple-element.89), channel_id=1, source_target_pairs={{2,4},{4,2},{6,8},{8,6},{10,12},{12,10},{3,5},{5,3},{7,9},{9,7},{1... | collective-permute-start | bytes 1990664 | tf_op jit(solution)/shard_map/ppermute | solution.py:1014
  138.7 6.9 %shard_map.217 = (f32[8,128,512]{2,1,0:T(8,128)}, f32[6,4,144,128]{3,2,1,0:T(8,128)S(1)}, f32[6,4,144,128]{3,2,1,0:T(8,128)S(1)}, f32[6,4,144,128]{3,2,1,0:T(8,1...) custom-call(s32[5]{0:T(128)S(1)} %convert_element_type.6.flags, ...), custom_call_target="tpu_custom_call" | custom-call | flops 805306368 | bytes 15925268 | tf_op jit(solution)/shard_map/pallas_call | solution.py:822
  145.6 1.5 collective-permute-done.4.rest_14_
  147.1 2.8 %shard_map.218 = (f32[8,128,512]{2,1,0:T(8,128)}, f32[4,64,256]{2,1,0:T(8,128)}) custom-call(s32[5]{0:T(128)S(1)} %convert_element_type.6.flags, f32[4,4,144,128]{3,2,1,0:T(8,128)S(1)} %get-tuple-element.72.edges.rest_0_, f32[2,2,4,144,128]{4,3,2,1,0:T(8,128)S(1)} %copy-done.4, ...), custom_call_target="tpu_custom_call", output_to_operand_aliasing={{0}: (17, {})} | custom-call | flops 15728640 | bytes 16105492 | tf_op jit(solution)/shard_map/pallas_call | solution.py:822
  (26 shorter events, 0.1 us)
Async XLA Ops:
  5.3 7.1 %copy-start = (bf16[8,128,512]{2,1,0:T(8,128)(2,1)S(1)}, bf16[8,128,512]{2,1,0:T(8,128)(2,1)}, u32[]{:S(2)}) copy-start(bf16[8,128,512]{2,1,0:T(8,128)(2,1)} %rest_0_.2) | copy-start | bytes 3145732
  5.3 7.1 %copy-start.5 = (bf16[512,256]{1,0:T(8,128)(2,1)S(1)}, bf16[512,256]{1,0:T(8,128)(2,1)}, u32[]{:S(2)}) copy-start(bf16[512,256]{1,0:T(8,128)(2,1)} %constant.81.clone.pairs) | copy-start | bytes 786436
  5.3 55.2 %all-to-all-start = ((f32[32,16,8,128]{3,2,1,0:T(8,128)}), f32[32,16,8,128]{3,2,1,0:T(8,128)S(1)}, u32[]{:S(2)}, u32[]{:S(2)}) async-start(f32[32,16,8,128]{3,2,1,0:T(8,128)} %bitcast.18), calls=%async_computation | async-start | bytes 4194304 | tf_op jit(solution)/shard_map/all_to_all | solution.py:911
  13.7 0.7 copy-start.6
  14.4 36.1 %collective-permute-start = (f32[160,512]{1,0:T(8,128)}, f32[160,512]{1,0:T(8,128)S(1)}, u32[]{:S(2)}, u32[]{:S(2)}) collective-permute-start(f32[160,512]{1,0:T(8,128)} %get-tuple-element.49), channel_id=1, source_target_pairs={{0,2},{2,4},{4,6},{6,8},{8,10},{10,12},{12,14},{1,3},{3,5},{5,7},{... | collective-permute-start | bytes 983048 | tf_op jit(solution)/shard_map/ppermute | solution.py:849
  17.9 32.6 %collective-permute-start.1 = (f32[160,512]{1,0:T(8,128)}, f32[160,512]{1,0:T(8,128)S(1)}, u32[]{:S(2)}, u32[]{:S(2)}) collective-permute-start(f32[160,512]{1,0:T(8,128)} %get-tuple-element.50), channel_id=1, source_target_pairs={{2,0},{4,2},{6,4},{8,6},{10,8},{12,10},{14,12},{3,1},{5,3},{7,5},{... | collective-permute-start | bytes 983048 | tf_op jit(solution)/shard_map/ppermute | solution.py:849
  19.9 4.5 %collective-permute-start.2 = (f32[16,512]{1,0:T(8,128)S(1)}, f32[16,512]{1,0:T(8,128)S(1)}, u32[]{:S(2)}, u32[]{:S(2)}) collective-permute-start(f32[16,512]{1,0:T(8,128)S(1)} %get-tuple-element.51), channel_id=1, source_target_pairs={{0,1},{1,16},{16,17},{2,3},{3,18},{18,19},{4,5},{5,20},{20,21},{6,... | collective-permute-start | bytes 98312 | tf_op jit(solution)/shard_map/ppermute | solution.py:849
  23.0 5.5 %collective-permute-start.3 = (f32[16,512]{1,0:T(8,128)S(1)}, f32[16,512]{1,0:T(8,128)S(1)}, u32[]{:S(2)}, u32[]{:S(2)}) collective-permute-start(f32[16,512]{1,0:T(8,128)S(1)} %get-tuple-element.52), channel_id=1, source_target_pairs={{1,0},{16,1},{17,16},{3,2},{18,3},{19,18},{5,4},{20,5},{21,20},{7,... | collective-permute-start | bytes 98312 | tf_op jit(solution)/shard_map/ppermute | solution.py:849
  24.4 43.5 %copy-start.9 = (f32[16,512]{1,0:T(8,128)}, f32[16,512]{1,0:T(8,128)S(1)}, u32[]{:S(2)}) copy-start(f32[16,512]{1,0:T(8,128)S(1)} %collective-permute-done.2.rest_4_) | copy-start | bytes 98308
  28.4 39.5 %copy-start.10 = (f32[16,512]{1,0:T(8,128)}, f32[16,512]{1,0:T(8,128)S(1)}, u32[]{:S(2)}) copy-start(f32[16,512]{1,0:T(8,128)S(1)} %collective-permute-done.3.rest_5_) | copy-start | bytes 98308
  50.5 17.4 %copy-start.7 = (f32[160,512]{1,0:T(8,128)}, f32[160,512]{1,0:T(8,128)S(1)}, u32[]{:S(2)}) copy-start(f32[160,512]{1,0:T(8,128)S(1)} %collective-permute-done.rest_2_) | copy-start | bytes 983044
  50.5 17.4 %copy-start.8 = (f32[160,512]{1,0:T(8,128)}, f32[160,512]{1,0:T(8,128)S(1)}, u32[]{:S(2)}) copy-start(f32[160,512]{1,0:T(8,128)S(1)} %collective-permute-done.1.rest_3_) | copy-start | bytes 983044
  67.9 63.5 %all-to-all-start.1 = ((f32[32,19,8,128]{3,2,1,0:T(8,128)}), f32[32,19,8,128]{3,2,1,0:T(8,128)S(1)}, u32[]{:S(2)}, u32[]{:S(2)}) async-start(f32[32,19,8,128]{3,2,1,0:T(8,128)} %shard_map.214), calls=%async_computation.1 | async-start | bytes 4980736 | tf_op jit(solution)/shard_map/all_to_all | solution.py:972
  76.7 1.2 copy-start.1
  77.9 1.0 copy-start.3
  131.4 7.3 %copy-start.2 = (f32[6,4,144,128]{3,2,1,0:T(8,128)S(1)}, f32[6,4,144,128]{3,2,1,0:T(8,128)}, u32[]{:S(2)}) copy-start(f32[6,4,144,128]{3,2,1,0:T(8,128)} %copy-done.1) | copy-start | bytes 5308420
  135.1 12.0 %collective-permute-start.4 = (f32[1296,128]{1,0:T(8,128)S(1)}, f32[1296,128]{1,0:T(8,128)S(1)}, u32[]{:S(2)}, u32[]{:S(2)}) collective-permute-start(f32[1296,128]{1,0:T(8,128)S(1)} %get-tuple-element.89), channel_id=1, source_target_pairs={{2,4},{4,2},{6,8},{8,6},{10,12},{12,10},{3,5},{5,3},{7,9},{9,7},{1... | collective-permute-start | bytes 1990664 | tf_op jit(solution)/shard_map/ppermute | solution.py:1014
  138.6 8.5 %collective-permute-start.5 = (f32[1296,128]{1,0:T(8,128)S(1)}, f32[1296,128]{1,0:T(8,128)S(1)}, u32[]{:S(2)}, u32[]{:S(2)}) collective-permute-start(f32[1296,128]{1,0:T(8,128)S(1)} %get-tuple-element.90), channel_id=1, source_target_pairs={{0,2},{2,0},{4,6},{6,4},{8,10},{10,8},{12,14},{14,12},{1,3},{3,1},... | collective-permute-start | bytes 1990664 | tf_op jit(solution)/shard_map/ppermute | solution.py:1014
  138.7 8.4 %copy-start.4 = (f32[2,2,4,144,128]{4,3,2,1,0:T(8,128)S(1)}, f32[2,2,4,144,128]{4,3,2,1,0:T(8,128)}, u32[]{:S(2)}) copy-start(f32[2,2,4,144,128]{4,3,2,1,0:T(8,128)} %copy-done.3) | copy-start | bytes 3538948

commit v4 on v3

--- a/solution.py
+++ b/solution.py
@@ -157,7 +157,8 @@
     pieces, rows = d.shape[0], d.shape[1] // 2
     parts = [slice(p * LANE, (p + 2) * LANE) for p in range(0, planes, 2)]
     pairs = [(x_hbm.at[at, :], x.at[at, :]) for at in parts]
-    copies = load([(d_hbm.at[0], d.at[0])] + pairs + [(d_hbm.at[i], d.at[i]) for i in range(1, pieces)], sems)
+    copies = load([(d_hbm.at[0], d.at[0])] + pairs, sems)
+    later = [(d_hbm.at[i], d.at[i]) for i in range(1, pieces)]
     sent = []
     copies[0].wait()
     for piece in range(pieces):
@@ -166,6 +167,8 @@
         for i, at in enumerate(parts):
             if piece == 0:
                 copies[i + 1].wait()
+            if piece == 0 and at is parts[-1]:
+                copies += send(later, sems, len(copies))
             value = dot_t(d[piece], x[at, :])
             value = value[:rows] + value[rows:]
             for h in range(2):
@@ -188,7 +191,7 @@
         rest[2 * count + 1 :],
     )
     out, sems, zh, zl, y, oh, ol, qh, ql = rest
-    copies = load(list(zip(away, near)), sems)
+    copies = load(list(zip(away, near))[:5], sems)
     csh, csl, forward, inverse, coarse_inverse, cch, ccl, ch, cl = near
     q_count = 2 * js
     half, quarter = second // 2, second // 4
@@ -203,9 +206,10 @@
                 lanes = slice(g * LANE, (g + 1) * LANE)
                 zh[0, at, lanes], zl[0, at, lanes] = split(near_half + far_half)
                 zh[1, at, lanes], zl[1, at, lanes] = split(near_half - far_half)
-    for copy in copies[:5]:
+    for copy in copies:
         copy.wait()
-    wide = 8 * first
+    copies = send(list(zip(away, near))[5:], sems, 5)
+    wide = 16 * first
     for top in range(0, q_count * first, wide):
         at = slice(top, top + wide)
         for parity in range(2):
@@ -269,7 +273,7 @@
             at = slice(j // 2 * first, (j // 2 + 1) * first)
             lanes = slice(j % 2 * half, (j % 2 + 1) * half)
             qh[at, lanes], ql[at, lanes] = split(operand)
-    for copy in copies[5:]:
+    for copy in copies:
         copy.wait()
     copies = []
     wide = 4 * first
@@ -381,7 +385,7 @@
     (devices, q_count, low, tiles, planes, length) = sizes
     away, (ks, cks, cols, far, near_edge), rest = rest[:7], rest[7:12], rest[12:]
     near, (lh, ll, mh, ml, sems) = rest[:7], rest[7:]
-    copies = load(list(zip(away, near)), sems)
+    copies = load(list(zip(away, near))[:4], sems)
     eh, el, ceh, cel, order, cwh, cwl = near
     cells, short = LANE, length // 2
     halves, coarse_planes = low // 2, planes // 2
@@ -399,8 +403,9 @@
         at = slice(n * LANE, (n + 1) * LANE)
         mh[at, :], ml[at, :] = split(jnp.transpose(rows))
 
-    for copy in copies[:4]:
+    for copy in copies:
         copy.wait()
+    copies = send(list(zip(away, near))[4:], sems, 4)
 
     for i in range(0, 4, 2):
         inverse_pair(i, lh, ll, eh, el, ks, i, cells)
@@ -411,7 +416,7 @@
         part = jnp.exp(part)
         put_rows(cks, n, SUB, part)
 
-    for copy in copies[4:]:
+    for copy in copies:
         copy.wait()
     lane = lax.broadcasted_iota(jnp.int32, (SUB, LANE), 1)
     tile_rows = [b[(s * tiles + tiles - 1) * SUB : (s + 1) * tiles * SUB, :] for s in range(devices)]

time: 150 us -> 151 us (level)
  no operation moved by 1% of the time
where the time goes in v4:
time: 151 us
  waiting for transfers between devices  90.1 us (60%)
  Pallas kernels  29 us (19%)
  starting transfers between devices  27.4 us (18%)
  local copies, waits for them, and re-layouts  3.15 us (2%)
    all_to_all x1, waiting for transfers between devices, fused_body(): got = lax.all_to_all(out, EVERY, split_axis=0, concat_axis=0, tiled=True)  52.5 us
    pallas_call x7, Pallas kernels, call(): pl.pallas_call(kernel, out_shape=outs, in_specs=specs, out_specs=out_spec...  29 us
    ppermute x4, waiting for transfers between devices, swap(): return (lax.ppermute(hi, axis, up), lax.ppermute(lo, axis, down))  26.1 us
    all_to_all x1, waiting for transfers between devices, fused_body(): lax.all_to_all(sent, EVERY, split_axis=0, concat_axis=0, tiled=True)  9.98 us
    ppermute x4, starting transfers between devices, swap(): return (lax.ppermute(hi, axis, up), lax.ppermute(lo, axis, down))  9.83 us
    all_to_all x1, starting transfers between devices, fused_body(): lax.all_to_all(sent, EVERY, split_axis=0, concat_axis=0, tiled=True)  7.1 us
    all_to_all x1, starting transfers between devices, fused_body(): got = lax.all_to_all(out, EVERY, split_axis=0, concat_axis=0, tiled=True)  6.91 us
    ppermute x2, starting transfers between devices, fused_body(): lax.ppermute(x, 'row', [p for i in range(at, rows - 1, 2) for p in ((i, i...  3.6 us
  transfers between devices with their start and end apart: 8, of which 5 were waited for; matrix products, arithmetic and copies ran while one was open for 0% of the time, Pallas kernels for 7%

profile of v4, /device:TPU:1, one launch (start us, length us, event | category | flops | bytes accessed | tf_op | source)
XLA Modules:
  0.0 150.5 jit_solution(9342304101507042941)
XLA Ops:
  0.6 5.3 %shard_map.212 = f32[4096,128]{1,0:T(8,128)} custom-call(bf16[4,256,512]{2,1,0:T(8,128)(2,1)} %constant.80.clone.d_hbm, bf16[1024,512]{1,0:T(8,128)(2,1)} %bitcast.19), custom_call_target="tpu_custom_call" | custom-call | flops 1073741824 | bytes 4194304 | tf_op jit(solution)/shard_map/pallas_call | solution.py:827
  5.9 7.1 %all-to-all-start = ((f32[32,16,8,128]{3,2,1,0:T(8,128)}), f32[32,16,8,128]{3,2,1,0:T(8,128)S(1)}, u32[]{:S(2)}, u32[]{:S(2)}) async-start(f32[32,16,8,128]{3,2,1,0:T(8,128)} %bitcast.18), calls=%async_computation | async-start | bytes 4194304 | tf_op jit(solution)/shard_map/all_to_all | solution.py:916
  13.1 1.3 shard_map.213
  14.3 0.7 copy-done.6
  15.0 3.5 %collective-permute-start = (f32[160,512]{1,0:T(8,128)}, f32[160,512]{1,0:T(8,128)S(1)}, u32[]{:S(2)}, u32[]{:S(2)}) collective-permute-start(f32[160,512]{1,0:T(8,128)} %get-tuple-element.49), channel_id=1, source_target_pairs={{0,2},{2,4},{4,6},{6,8},{8,10},{10,12},{12,14},{1,3},{3,5},{5,7},{... | collective-permute-start | bytes 983048 | tf_op jit(solution)/shard_map/ppermute | solution.py:854
  18.6 1.9 %collective-permute-start.1 = (f32[160,512]{1,0:T(8,128)}, f32[160,512]{1,0:T(8,128)S(1)}, u32[]{:S(2)}, u32[]{:S(2)}) collective-permute-start(f32[160,512]{1,0:T(8,128)} %get-tuple-element.50), channel_id=1, source_target_pairs={{2,0},{4,2},{6,4},{8,6},{10,8},{12,10},{14,12},{3,1},{5,3},{7,5},{... | collective-permute-start | bytes 983048 | tf_op jit(solution)/shard_map/ppermute | solution.py:854
  20.5 3.1 %collective-permute-start.2 = (f32[16,512]{1,0:T(8,128)S(1)}, f32[16,512]{1,0:T(8,128)S(1)}, u32[]{:S(2)}, u32[]{:S(2)}) collective-permute-start(f32[16,512]{1,0:T(8,128)S(1)} %get-tuple-element.51), channel_id=1, source_target_pairs={{0,1},{1,16},{16,17},{2,3},{3,18},{18,19},{4,5},{5,20},{20,21},{6,... | collective-permute-start | bytes 98312 | tf_op jit(solution)/shard_map/ppermute | solution.py:854
  23.6 1.3 collective-permute-start.3
  24.9 0.1 copy.26.scale
  25.0 4.0 %collective-permute-done.3.rest_5_ = f32[16,512]{1,0:T(8,128)S(1)} collective-permute-done((f32[16,512]{1,0:T(8,128)S(1)}, f32[16,512]{1,0:T(8,128)S(1)}, u32[]{:S(2)}, u32[]{:S(2)}) %collective-permute-start.3) | collective-permute-done | bytes 32800 | tf_op jit(solution)/shard_map/ppermute | solution.py:854
  29.1 22.1 %collective-permute-done.rest_2_ = f32[160,512]{1,0:T(8,128)S(1)} collective-permute-done((f32[160,512]{1,0:T(8,128)}, f32[160,512]{1,0:T(8,128)S(1)}, u32[]{:S(2)}, u32[]{:S(2)}) %collective-permute-start) | collective-permute-done | bytes 327712 | tf_op jit(solution)/shard_map/ppermute | solution.py:854
  51.2 10.0 %all-to-all-done.b = f32[32,16,8,128]{3,2,1,0:T(8,128)S(1)} async-done(((f32[32,16,8,128]{3,2,1,0:T(8,128)}), f32[32,16,8,128]{3,2,1,0:T(8,128)S(1)}, u32[]{:S(2)}, u32[]{:S(2)}) %all-to-all-start) | async-done | bytes 2097184 | tf_op jit(solution)/shard_map/all_to_all | solution.py:916
  61.1 7.3 %shard_map.214 = f32[32,19,8,128]{3,2,1,0:T(8,128)} custom-call(f32[8,2]{1,0:T(8,128)S(1)} %copy.26.scale, f32[32,16,8,128]{3,2,1,0:T(8,128)S(1)} %all-to-all-done.b, bf16[2,256,256]{2,1,0:T(8,128)(2,1)} %constant.83.clone.rest_0_, bf16[2,256,256]{2,1,0:T(8,128)(2,1)} %constant.84.clone.rest_1_, bf16[256,256]{1,0:T(8,128)(2,1)} %constant.85.clone.rest_2_, ...), custom_call_target="tpu_custom_call" | custom-call | flops 4026531840 | bytes 7012416 | tf_op jit(solution)/shard_map/pallas_call | solution.py:827
  68.5 6.9 %all-to-all-start.1 = ((f32[32,19,8,128]{3,2,1,0:T(8,128)}), f32[32,19,8,128]{3,2,1,0:T(8,128)S(1)}, u32[]{:S(2)}, u32[]{:S(2)}) async-start(f32[32,19,8,128]{3,2,1,0:T(8,128)} %shard_map.214), calls=%async_computation.1 | async-start | bytes 4980736 | tf_op jit(solution)/shard_map/all_to_all | solution.py:977
  75.5 0.1 stack.32
  75.6 1.7 %shard_map.215 = (f32[6,4,144,128]{3,2,1,0:T(8,128)S(1)}, f32[2,2,4,144,128]{4,3,2,1,0:T(8,128)S(1)}, f32[2,2,80,128]{3,2,1,0:T(8,128)S(1)}, f32[2,2,2,80,128]{4,3,2,1,0:T(8,128)S(1)}) custom-call(bf16[8,128,512]{2,1,0:T(8,128)(2,1)} %rest_0_.2, f32[4,64,256]{2,1,0:T(8,128)} %bitcast.17, f32[160,512]{1,0:T(8,128)} %copy-done.7, f32[160,512]{1,0:T(8,128)} %copy-done.8, ...), custom_call_target="tpu_custom_call" | custom-call | flops 524288 | bytes 5472256 | tf_op jit(solution)/shard_map/pallas_call | solution.py:827
  77.3 1.2 copy-done.1
  78.5 1.0 copy-done.3
  79.6 52.5 %all-to-all-done.1 = f32[32,19,8,128]{3,2,1,0:T(8,128)S(1)} async-done(((f32[32,19,8,128]{3,2,1,0:T(8,128)}), f32[32,19,8,128]{3,2,1,0:T(8,128)S(1)}, u32[]{:S(2)}, u32[]{:S(2)}) %all-to-all-start.1) | async-done | bytes 2490400 | tf_op jit(solution)/shard_map/all_to_all | solution.py:977
  132.0 3.7 %shard_map.216 = (f32[4,4,144,128]{3,2,1,0:T(8,128)S(1)}, f32[4,2,80,128]{3,2,1,0:T(8,128)S(1)}, f32[32,512]{1,0:T(8,128)S(1)}, f32[1296,128]{1,0:T(8,128)S(1)}, f32[1296,128]{1,0:T(8,128)S(1)}) custom-call(s32[5]{0:T(128)S(1)} %convert_element_type.6.flags, f32[4864,128]{1,0:T(8,128)S(1)} %bitcast.14, bf16[2,256,256]{2,1,0:T(8,128)(2,1)} %constant.92.clone.rest_0_.eh_hbm, ...), custom_call_target="tpu_custom_call" | custom-call | flops 805306368 | bytes 6471700 | tf_op jit(solution)/shard_map/pallas_call | solution.py:827
  135.7 3.5 %collective-permute-start.4 = (f32[1296,128]{1,0:T(8,128)S(1)}, f32[1296,128]{1,0:T(8,128)S(1)}, u32[]{:S(2)}, u32[]{:S(2)}) collective-permute-start(f32[1296,128]{1,0:T(8,128)S(1)} %get-tuple-element.89), channel_id=1, source_target_pairs={{2,4},{4,2},{6,8},{8,6},{10,12},{12,10},{3,5},{5,3},{7,9},{9,7},{1... | collective-permute-start | bytes 1990664 | tf_op jit(solution)/shard_map/ppermute | solution.py:1019
  139.4 6.9 %shard_map.217 = (f32[8,128,512]{2,1,0:T(8,128)}, f32[6,4,144,128]{3,2,1,0:T(8,128)S(1)}, f32[6,4,144,128]{3,2,1,0:T(8,128)S(1)}, f32[6,4,144,128]{3,2,1,0:T(8,1...) custom-call(s32[5]{0:T(128)S(1)} %convert_element_type.6.flags, ...), custom_call_target="tpu_custom_call" | custom-call | flops 805306368 | bytes 15925268 | tf_op jit(solution)/shard_map/pallas_call | solution.py:827
  146.2 1.5 collective-permute-done.4.rest_14_
  147.7 2.8 %shard_map.218 = (f32[8,128,512]{2,1,0:T(8,128)}, f32[4,64,256]{2,1,0:T(8,128)}) custom-call(s32[5]{0:T(128)S(1)} %convert_element_type.6.flags, f32[4,4,144,128]{3,2,1,0:T(8,128)S(1)} %get-tuple-element.72.edges.rest_0_, f32[2,2,4,144,128]{4,3,2,1,0:T(8,128)S(1)} %copy-done.4, ...), custom_call_target="tpu_custom_call", output_to_operand_aliasing={{0}: (17, {})} | custom-call | flops 15728640 | bytes 16105492 | tf_op jit(solution)/shard_map/pallas_call | solution.py:827
  (26 shorter events, 0.1 us)
Async XLA Ops:
  5.9 7.1 %copy-start = (bf16[8,128,512]{2,1,0:T(8,128)(2,1)S(1)}, bf16[8,128,512]{2,1,0:T(8,128)(2,1)}, u32[]{:S(2)}) copy-start(bf16[8,128,512]{2,1,0:T(8,128)(2,1)} %rest_0_.2) | copy-start | bytes 3145732
  5.9 7.1 %copy-start.5 = (bf16[512,256]{1,0:T(8,128)(2,1)S(1)}, bf16[512,256]{1,0:T(8,128)(2,1)}, u32[]{:S(2)}) copy-start(bf16[512,256]{1,0:T(8,128)(2,1)} %constant.81.clone.pairs) | copy-start | bytes 786436
  5.9 55.2 %all-to-all-start = ((f32[32,16,8,128]{3,2,1,0:T(8,128)}), f32[32,16,8,128]{3,2,1,0:T(8,128)S(1)}, u32[]{:S(2)}, u32[]{:S(2)}) async-start(f32[32,16,8,128]{3,2,1,0:T(8,128)} %bitcast.18), calls=%async_computation | async-start | bytes 4194304 | tf_op jit(solution)/shard_map/all_to_all | solution.py:916
  14.3 0.7 copy-start.6
  15.0 36.1 %collective-permute-start = (f32[160,512]{1,0:T(8,128)}, f32[160,512]{1,0:T(8,128)S(1)}, u32[]{:S(2)}, u32[]{:S(2)}) collective-permute-start(f32[160,512]{1,0:T(8,128)} %get-tuple-element.49), channel_id=1, source_target_pairs={{0,2},{2,4},{4,6},{6,8},{8,10},{10,12},{12,14},{1,3},{3,5},{5,7},{... | collective-permute-start | bytes 983048 | tf_op jit(solution)/shard_map/ppermute | solution.py:854
  18.6 32.6 %collective-permute-start.1 = (f32[160,512]{1,0:T(8,128)}, f32[160,512]{1,0:T(8,128)S(1)}, u32[]{:S(2)}, u32[]{:S(2)}) collective-permute-start(f32[160,512]{1,0:T(8,128)} %get-tuple-element.50), channel_id=1, source_target_pairs={{2,0},{4,2},{6,4},{8,6},{10,8},{12,10},{14,12},{3,1},{5,3},{7,5},{... | collective-permute-start | bytes 983048 | tf_op jit(solution)/shard_map/ppermute | solution.py:854
  20.5 4.5 %collective-permute-start.2 = (f32[16,512]{1,0:T(8,128)S(1)}, f32[16,512]{1,0:T(8,128)S(1)}, u32[]{:S(2)}, u32[]{:S(2)}) collective-permute-start(f32[16,512]{1,0:T(8,128)S(1)} %get-tuple-element.51), channel_id=1, source_target_pairs={{0,1},{1,16},{16,17},{2,3},{3,18},{18,19},{4,5},{5,20},{20,21},{6,... | collective-permute-start | bytes 98312 | tf_op jit(solution)/shard_map/ppermute | solution.py:854
  23.6 5.5 %collective-permute-start.3 = (f32[16,512]{1,0:T(8,128)S(1)}, f32[16,512]{1,0:T(8,128)S(1)}, u32[]{:S(2)}, u32[]{:S(2)}) collective-permute-start(f32[16,512]{1,0:T(8,128)S(1)} %get-tuple-element.52), channel_id=1, source_target_pairs={{1,0},{16,1},{17,16},{3,2},{18,3},{19,18},{5,4},{20,5},{21,20},{7,... | collective-permute-start | bytes 98312 | tf_op jit(solution)/shard_map/ppermute | solution.py:854
  25.0 43.5 %copy-start.9 = (f32[16,512]{1,0:T(8,128)}, f32[16,512]{1,0:T(8,128)S(1)}, u32[]{:S(2)}) copy-start(f32[16,512]{1,0:T(8,128)S(1)} %collective-permute-done.2.rest_4_) | copy-start | bytes 98308
  29.1 39.5 %copy-start.10 = (f32[16,512]{1,0:T(8,128)}, f32[16,512]{1,0:T(8,128)S(1)}, u32[]{:S(2)}) copy-start(f32[16,512]{1,0:T(8,128)S(1)} %collective-permute-done.3.rest_5_) | copy-start | bytes 98308
  51.2 17.4 %copy-start.7 = (f32[160,512]{1,0:T(8,128)}, f32[160,512]{1,0:T(8,128)S(1)}, u32[]{:S(2)}) copy-start(f32[160,512]{1,0:T(8,128)S(1)} %collective-permute-done.rest_2_) | copy-start | bytes 983044
  51.2 17.4 %copy-start.8 = (f32[160,512]{1,0:T(8,128)}, f32[160,512]{1,0:T(8,128)S(1)}, u32[]{:S(2)}) copy-start(f32[160,512]{1,0:T(8,128)S(1)} %collective-permute-done.1.rest_3_) | copy-start | bytes 983044
  68.5 63.5 %all-to-all-start.1 = ((f32[32,19,8,128]{3,2,1,0:T(8,128)}), f32[32,19,8,128]{3,2,1,0:T(8,128)S(1)}, u32[]{:S(2)}, u32[]{:S(2)}) async-start(f32[32,19,8,128]{3,2,1,0:T(8,128)} %shard_map.214), calls=%async_computation.1 | async-start | bytes 4980736 | tf_op jit(solution)/shard_map/all_to_all | solution.py:977
  77.3 1.2 copy-start.1
  78.5 1.0 copy-start.3
  132.0 7.3 %copy-start.2 = (f32[6,4,144,128]{3,2,1,0:T(8,128)S(1)}, f32[6,4,144,128]{3,2,1,0:T(8,128)}, u32[]{:S(2)}) copy-start(f32[6,4,144,128]{3,2,1,0:T(8,128)} %copy-done.1) | copy-start | bytes 5308420
  135.7 12.0 %collective-permute-start.4 = (f32[1296,128]{1,0:T(8,128)S(1)}, f32[1296,128]{1,0:T(8,128)S(1)}, u32[]{:S(2)}, u32[]{:S(2)}) collective-permute-start(f32[1296,128]{1,0:T(8,128)S(1)} %get-tuple-element.89), channel_id=1, source_target_pairs={{2,4},{4,2},{6,8},{8,6},{10,12},{12,10},{3,5},{5,3},{7,9},{9,7},{1... | collective-permute-start | bytes 1990664 | tf_op jit(solution)/shard_map/ppermute | solution.py:1019
  139.3 8.5 %collective-permute-start.5 = (f32[1296,128]{1,0:T(8,128)S(1)}, f32[1296,128]{1,0:T(8,128)S(1)}, u32[]{:S(2)}, u32[]{:S(2)}) collective-permute-start(f32[1296,128]{1,0:T(8,128)S(1)} %get-tuple-element.90), channel_id=1, source_target_pairs={{0,2},{2,0},{4,6},{6,4},{8,10},{10,8},{12,14},{14,12},{1,3},{3,1},... | collective-permute-start | bytes 1990664 | tf_op jit(solution)/shard_map/ppermute | solution.py:1019
  139.3 8.4 %copy-start.4 = (f32[2,2,4,144,128]{4,3,2,1,0:T(8,128)S(1)}, f32[2,2,4,144,128]{4,3,2,1,0:T(8,128)}, u32[]{:S(2)}) copy-start(f32[2,2,4,144,128]{4,3,2,1,0:T(8,128)} %copy-done.3) | copy-start | bytes 3538948

commit v5 on v4

--- a/solution.py
+++ b/solution.py
@@ -157,8 +157,7 @@
     pieces, rows = d.shape[0], d.shape[1] // 2
     parts = [slice(p * LANE, (p + 2) * LANE) for p in range(0, planes, 2)]
     pairs = [(x_hbm.at[at, :], x.at[at, :]) for at in parts]
-    copies = load([(d_hbm.at[0], d.at[0])] + pairs, sems)
-    later = [(d_hbm.at[i], d.at[i]) for i in range(1, pieces)]
+    copies = load([(d_hbm.at[0], d.at[0])] + pairs + [(d_hbm.at[i], d.at[i]) for i in range(1, pieces)], sems)
     sent = []
     copies[0].wait()
     for piece in range(pieces):
@@ -167,8 +166,6 @@
         for i, at in enumerate(parts):
             if piece == 0:
                 copies[i + 1].wait()
-            if piece == 0 and at is parts[-1]:
-                copies += send(later, sems, len(copies))
             value = dot_t(d[piece], x[at, :])
             value = value[:rows] + value[rows:]
             for h in range(2):

time: 151 us -> 150 us (level)
  no operation moved by 1% of the time
where the time goes in v5:
time: 150 us
  waiting for transfers between devices  90.1 us (60%)
  Pallas kernels  28.3 us (19%)
  starting transfers between devices  27.5 us (18%)
  local copies, waits for them, and re-layouts  3.15 us (2%)
    all_to_all x1, waiting for transfers between devices, fused_body(): got = lax.all_to_all(out, EVERY, split_axis=0, concat_axis=0, tiled=True)  52.5 us
    pallas_call x7, Pallas kernels, call(): pl.pallas_call(kernel, out_shape=outs, in_specs=specs, out_specs=out_spec...  28.3 us
    ppermute x4, waiting for transfers between devices, swap(): return (lax.ppermute(hi, axis, up), lax.ppermute(lo, axis, down))  26.1 us
    all_to_all x1, waiting for transfers between devices, fused_body(): lax.all_to_all(sent, EVERY, split_axis=0, concat_axis=0, tiled=True)  9.98 us
    ppermute x4, starting transfers between devices, swap(): return (lax.ppermute(hi, axis, up), lax.ppermute(lo, axis, down))  9.83 us
    all_to_all x1, starting transfers between devices, fused_body(): lax.all_to_all(sent, EVERY, split_axis=0, concat_axis=0, tiled=True)  7.1 us
    all_to_all x1, starting transfers between devices, fused_body(): got = lax.all_to_all(out, EVERY, split_axis=0, concat_axis=0, tiled=True)  6.92 us
    ppermute x2, starting transfers between devices, fused_body(): lax.ppermute(x, 'row', [p for i in range(at, rows - 1, 2) for p in ((i, i...  3.6 us
  transfers between devices with their start and end apart: 8, of which 5 were waited for; matrix products, arithmetic and copies ran while one was open for 0% of the time, Pallas kernels for 7%

profile of v5, /device:TPU:1, one launch (start us, length us, event | category | flops | bytes accessed | tf_op | source)
XLA Modules:
  0.0 149.9 jit_solution(8826747937920260353)
XLA Ops:
  0.6 4.6 %shard_map.212 = f32[4096,128]{1,0:T(8,128)} custom-call(bf16[4,256,512]{2,1,0:T(8,128)(2,1)} %constant.80.clone.d_hbm, bf16[1024,512]{1,0:T(8,128)(2,1)} %bitcast.19), custom_call_target="tpu_custom_call" | custom-call | flops 1073741824 | bytes 4194304 | tf_op jit(solution)/shard_map/pallas_call | solution.py:824
  5.3 7.1 %all-to-all-start = ((f32[32,16,8,128]{3,2,1,0:T(8,128)}), f32[32,16,8,128]{3,2,1,0:T(8,128)S(1)}, u32[]{:S(2)}, u32[]{:S(2)}) async-start(f32[32,16,8,128]{3,2,1,0:T(8,128)} %bitcast.18), calls=%async_computation | async-start | bytes 4194304 | tf_op jit(solution)/shard_map/all_to_all | solution.py:913
  12.4 1.3 shard_map.213
  13.7 0.7 copy-done.6
  14.4 3.5 %collective-permute-start = (f32[160,512]{1,0:T(8,128)}, f32[160,512]{1,0:T(8,128)S(1)}, u32[]{:S(2)}, u32[]{:S(2)}) collective-permute-start(f32[160,512]{1,0:T(8,128)} %get-tuple-element.49), channel_id=1, source_target_pairs={{0,2},{2,4},{4,6},{6,8},{8,10},{10,12},{12,14},{1,3},{3,5},{5,7},{... | collective-permute-start | bytes 983048 | tf_op jit(solution)/shard_map/ppermute | solution.py:851
  17.9 1.9 %collective-permute-start.1 = (f32[160,512]{1,0:T(8,128)}, f32[160,512]{1,0:T(8,128)S(1)}, u32[]{:S(2)}, u32[]{:S(2)}) collective-permute-start(f32[160,512]{1,0:T(8,128)} %get-tuple-element.50), channel_id=1, source_target_pairs={{2,0},{4,2},{6,4},{8,6},{10,8},{12,10},{14,12},{3,1},{5,3},{7,5},{... | collective-permute-start | bytes 983048 | tf_op jit(solution)/shard_map/ppermute | solution.py:851
  19.9 3.1 %collective-permute-start.2 = (f32[16,512]{1,0:T(8,128)S(1)}, f32[16,512]{1,0:T(8,128)S(1)}, u32[]{:S(2)}, u32[]{:S(2)}) collective-permute-start(f32[16,512]{1,0:T(8,128)S(1)} %get-tuple-element.51), channel_id=1, source_target_pairs={{0,1},{1,16},{16,17},{2,3},{3,18},{18,19},{4,5},{5,20},{20,21},{6,... | collective-permute-start | bytes 98312 | tf_op jit(solution)/shard_map/ppermute | solution.py:851
  23.0 1.3 collective-permute-start.3
  24.3 0.1 copy.26.scale
  24.4 4.0 %collective-permute-done.3.rest_5_ = f32[16,512]{1,0:T(8,128)S(1)} collective-permute-done((f32[16,512]{1,0:T(8,128)S(1)}, f32[16,512]{1,0:T(8,128)S(1)}, u32[]{:S(2)}, u32[]{:S(2)}) %collective-permute-start.3) | collective-permute-done | bytes 32800 | tf_op jit(solution)/shard_map/ppermute | solution.py:851
  28.4 22.1 %collective-permute-done.rest_2_ = f32[160,512]{1,0:T(8,128)S(1)} collective-permute-done((f32[160,512]{1,0:T(8,128)}, f32[160,512]{1,0:T(8,128)S(1)}, u32[]{:S(2)}, u32[]{:S(2)}) %collective-permute-start) | collective-permute-done | bytes 327712 | tf_op jit(solution)/shard_map/ppermute | solution.py:851
  50.5 10.0 %all-to-all-done.b = f32[32,16,8,128]{3,2,1,0:T(8,128)S(1)} async-done(((f32[32,16,8,128]{3,2,1,0:T(8,128)}), f32[32,16,8,128]{3,2,1,0:T(8,128)S(1)}, u32[]{:S(2)}, u32[]{:S(2)}) %all-to-all-start) | async-done | bytes 2097184 | tf_op jit(solution)/shard_map/all_to_all | solution.py:913
  60.5 7.3 %shard_map.214 = f32[32,19,8,128]{3,2,1,0:T(8,128)} custom-call(f32[8,2]{1,0:T(8,128)S(1)} %copy.26.scale, f32[32,16,8,128]{3,2,1,0:T(8,128)S(1)} %all-to-all-done.b, bf16[2,256,256]{2,1,0:T(8,128)(2,1)} %constant.83.clone.rest_0_, bf16[2,256,256]{2,1,0:T(8,128)(2,1)} %constant.84.clone.rest_1_, bf16[256,256]{1,0:T(8,128)(2,1)} %constant.85.clone.rest_2_, ...), custom_call_target="tpu_custom_call" | custom-call | flops 4026531840 | bytes 7012416 | tf_op jit(solution)/shard_map/pallas_call | solution.py:824
  67.9 6.9 %all-to-all-start.1 = ((f32[32,19,8,128]{3,2,1,0:T(8,128)}), f32[32,19,8,128]{3,2,1,0:T(8,128)S(1)}, u32[]{:S(2)}, u32[]{:S(2)}) async-start(f32[32,19,8,128]{3,2,1,0:T(8,128)} %shard_map.214), calls=%async_computation.1 | async-start | bytes 4980736 | tf_op jit(solution)/shard_map/all_to_all | solution.py:974
  74.8 0.1 stack.32
  74.9 1.7 %shard_map.215 = (f32[6,4,144,128]{3,2,1,0:T(8,128)S(1)}, f32[2,2,4,144,128]{4,3,2,1,0:T(8,128)S(1)}, f32[2,2,80,128]{3,2,1,0:T(8,128)S(1)}, f32[2,2,2,80,128]{4,3,2,1,0:T(8,128)S(1)}) custom-call(bf16[8,128,512]{2,1,0:T(8,128)(2,1)} %rest_0_.2, f32[4,64,256]{2,1,0:T(8,128)} %bitcast.17, f32[160,512]{1,0:T(8,128)} %copy-done.7, f32[160,512]{1,0:T(8,128)} %copy-done.8, ...), custom_call_target="tpu_custom_call" | custom-call | flops 524288 | bytes 5472256 | tf_op jit(solution)/shard_map/pallas_call | solution.py:824
  76.7 1.2 copy-done.1
  77.9 1.0 copy-done.3
  78.9 52.5 %all-to-all-done.1 = f32[32,19,8,128]{3,2,1,0:T(8,128)S(1)} async-done(((f32[32,19,8,128]{3,2,1,0:T(8,128)}), f32[32,19,8,128]{3,2,1,0:T(8,128)S(1)}, u32[]{:S(2)}, u32[]{:S(2)}) %all-to-all-start.1) | async-done | bytes 2490400 | tf_op jit(solution)/shard_map/all_to_all | solution.py:974
  131.4 3.7 %shard_map.216 = (f32[4,4,144,128]{3,2,1,0:T(8,128)S(1)}, f32[4,2,80,128]{3,2,1,0:T(8,128)S(1)}, f32[32,512]{1,0:T(8,128)S(1)}, f32[1296,128]{1,0:T(8,128)S(1)}, f32[1296,128]{1,0:T(8,128)S(1)}) custom-call(s32[5]{0:T(128)S(1)} %convert_element_type.6.flags, f32[4864,128]{1,0:T(8,128)S(1)} %bitcast.14, bf16[2,256,256]{2,1,0:T(8,128)(2,1)} %constant.92.clone.rest_0_.eh_hbm, ...), custom_call_target="tpu_custom_call" | custom-call | flops 805306368 | bytes 6471700 | tf_op jit(solution)/shard_map/pallas_call | solution.py:824
  135.1 3.5 %collective-permute-start.4 = (f32[1296,128]{1,0:T(8,128)S(1)}, f32[1296,128]{1,0:T(8,128)S(1)}, u32[]{:S(2)}, u32[]{:S(2)}) collective-permute-start(f32[1296,128]{1,0:T(8,128)S(1)} %get-tuple-element.89), channel_id=1, source_target_pairs={{2,4},{4,2},{6,8},{8,6},{10,12},{12,10},{3,5},{5,3},{7,9},{9,7},{1... | collective-permute-start | bytes 1990664 | tf_op jit(solution)/shard_map/ppermute | solution.py:1016
  138.7 6.9 %shard_map.217 = (f32[8,128,512]{2,1,0:T(8,128)}, f32[6,4,144,128]{3,2,1,0:T(8,128)S(1)}, f32[6,4,144,128]{3,2,1,0:T(8,128)S(1)}, f32[6,4,144,128]{3,2,1,0:T(8,1...) custom-call(s32[5]{0:T(128)S(1)} %convert_element_type.6.flags, ...), custom_call_target="tpu_custom_call" | custom-call | flops 805306368 | bytes 15925268 | tf_op jit(solution)/shard_map/pallas_call | solution.py:824
  145.6 1.5 collective-permute-done.4.rest_14_
  147.1 2.8 %shard_map.218 = (f32[8,128,512]{2,1,0:T(8,128)}, f32[4,64,256]{2,1,0:T(8,128)}) custom-call(s32[5]{0:T(128)S(1)} %convert_element_type.6.flags, f32[4,4,144,128]{3,2,1,0:T(8,128)S(1)} %get-tuple-element.72.edges.rest_0_, f32[2,2,4,144,128]{4,3,2,1,0:T(8,128)S(1)} %copy-done.4, ...), custom_call_target="tpu_custom_call", output_to_operand_aliasing={{0}: (17, {})} | custom-call | flops 15728640 | bytes 16105492 | tf_op jit(solution)/shard_map/pallas_call | solution.py:824
  (26 shorter events, 0.1 us)
Async XLA Ops:
  5.3 7.1 %copy-start = (bf16[8,128,512]{2,1,0:T(8,128)(2,1)S(1)}, bf16[8,128,512]{2,1,0:T(8,128)(2,1)}, u32[]{:S(2)}) copy-start(bf16[8,128,512]{2,1,0:T(8,128)(2,1)} %rest_0_.2) | copy-start | bytes 3145732
  5.3 7.1 %copy-start.5 = (bf16[512,256]{1,0:T(8,128)(2,1)S(1)}, bf16[512,256]{1,0:T(8,128)(2,1)}, u32[]{:S(2)}) copy-start(bf16[512,256]{1,0:T(8,128)(2,1)} %constant.81.clone.pairs) | copy-start | bytes 786436
  5.3 55.2 %all-to-all-start = ((f32[32,16,8,128]{3,2,1,0:T(8,128)}), f32[32,16,8,128]{3,2,1,0:T(8,128)S(1)}, u32[]{:S(2)}, u32[]{:S(2)}) async-start(f32[32,16,8,128]{3,2,1,0:T(8,128)} %bitcast.18), calls=%async_computation | async-start | bytes 4194304 | tf_op jit(solution)/shard_map/all_to_all | solution.py:913
  13.7 0.7 copy-start.6
  14.4 36.1 %collective-permute-start = (f32[160,512]{1,0:T(8,128)}, f32[160,512]{1,0:T(8,128)S(1)}, u32[]{:S(2)}, u32[]{:S(2)}) collective-permute-start(f32[160,512]{1,0:T(8,128)} %get-tuple-element.49), channel_id=1, source_target_pairs={{0,2},{2,4},{4,6},{6,8},{8,10},{10,12},{12,14},{1,3},{3,5},{5,7},{... | collective-permute-start | bytes 983048 | tf_op jit(solution)/shard_map/ppermute | solution.py:851
  17.9 32.6 %collective-permute-start.1 = (f32[160,512]{1,0:T(8,128)}, f32[160,512]{1,0:T(8,128)S(1)}, u32[]{:S(2)}, u32[]{:S(2)}) collective-permute-start(f32[160,512]{1,0:T(8,128)} %get-tuple-element.50), channel_id=1, source_target_pairs={{2,0},{4,2},{6,4},{8,6},{10,8},{12,10},{14,12},{3,1},{5,3},{7,5},{... | collective-permute-start | bytes 983048 | tf_op jit(solution)/shard_map/ppermute | solution.py:851
  19.9 4.5 %collective-permute-start.2 = (f32[16,512]{1,0:T(8,128)S(1)}, f32[16,512]{1,0:T(8,128)S(1)}, u32[]{:S(2)}, u32[]{:S(2)}) collective-permute-start(f32[16,512]{1,0:T(8,128)S(1)} %get-tuple-element.51), channel_id=1, source_target_pairs={{0,1},{1,16},{16,17},{2,3},{3,18},{18,19},{4,5},{5,20},{20,21},{6,... | collective-permute-start | bytes 98312 | tf_op jit(solution)/shard_map/ppermute | solution.py:851
  23.0 5.5 %collective-permute-start.3 = (f32[16,512]{1,0:T(8,128)S(1)}, f32[16,512]{1,0:T(8,128)S(1)}, u32[]{:S(2)}, u32[]{:S(2)}) collective-permute-start(f32[16,512]{1,0:T(8,128)S(1)} %get-tuple-element.52), channel_id=1, source_target_pairs={{1,0},{16,1},{17,16},{3,2},{18,3},{19,18},{5,4},{20,5},{21,20},{7,... | collective-permute-start | bytes 98312 | tf_op jit(solution)/shard_map/ppermute | solution.py:851
  24.4 43.5 %copy-start.9 = (f32[16,512]{1,0:T(8,128)}, f32[16,512]{1,0:T(8,128)S(1)}, u32[]{:S(2)}) copy-start(f32[16,512]{1,0:T(8,128)S(1)} %collective-permute-done.2.rest_4_) | copy-start | bytes 98308
  28.4 39.4 %copy-start.10 = (f32[16,512]{1,0:T(8,128)}, f32[16,512]{1,0:T(8,128)S(1)}, u32[]{:S(2)}) copy-start(f32[16,512]{1,0:T(8,128)S(1)} %collective-permute-done.3.rest_5_) | copy-start | bytes 98308
  50.5 17.4 %copy-start.7 = (f32[160,512]{1,0:T(8,128)}, f32[160,512]{1,0:T(8,128)S(1)}, u32[]{:S(2)}) copy-start(f32[160,512]{1,0:T(8,128)S(1)} %collective-permute-done.rest_2_) | copy-start | bytes 983044
  50.5 17.4 %copy-start.8 = (f32[160,512]{1,0:T(8,128)}, f32[160,512]{1,0:T(8,128)S(1)}, u32[]{:S(2)}) copy-start(f32[160,512]{1,0:T(8,128)S(1)} %collective-permute-done.1.rest_3_) | copy-start | bytes 983044
  67.9 63.5 %all-to-all-start.1 = ((f32[32,19,8,128]{3,2,1,0:T(8,128)}), f32[32,19,8,128]{3,2,1,0:T(8,128)S(1)}, u32[]{:S(2)}, u32[]{:S(2)}) async-start(f32[32,19,8,128]{3,2,1,0:T(8,128)} %shard_map.214), calls=%async_computation.1 | async-start | bytes 4980736 | tf_op jit(solution)/shard_map/all_to_all | solution.py:974
  76.7 1.2 copy-start.1
  77.9 1.0 copy-start.3
  131.4 7.3 %copy-start.2 = (f32[6,4,144,128]{3,2,1,0:T(8,128)S(1)}, f32[6,4,144,128]{3,2,1,0:T(8,128)}, u32[]{:S(2)}) copy-start(f32[6,4,144,128]{3,2,1,0:T(8,128)} %copy-done.1) | copy-start | bytes 5308420
  135.1 12.0 %collective-permute-start.4 = (f32[1296,128]{1,0:T(8,128)S(1)}, f32[1296,128]{1,0:T(8,128)S(1)}, u32[]{:S(2)}, u32[]{:S(2)}) collective-permute-start(f32[1296,128]{1,0:T(8,128)S(1)} %get-tuple-element.89), channel_id=1, source_target_pairs={{2,4},{4,2},{6,8},{8,6},{10,12},{12,10},{3,5},{5,3},{7,9},{9,7},{1... | collective-permute-start | bytes 1990664 | tf_op jit(solution)/shard_map/ppermute | solution.py:1016
  138.6 8.5 %collective-permute-start.5 = (f32[1296,128]{1,0:T(8,128)S(1)}, f32[1296,128]{1,0:T(8,128)S(1)}, u32[]{:S(2)}, u32[]{:S(2)}) collective-permute-start(f32[1296,128]{1,0:T(8,128)S(1)} %get-tuple-element.90), channel_id=1, source_target_pairs={{0,2},{2,0},{4,6},{6,4},{8,10},{10,8},{12,14},{14,12},{1,3},{3,1},... | collective-permute-start | bytes 1990664 | tf_op jit(solution)/shard_map/ppermute | solution.py:1016
  138.7 8.4 %copy-start.4 = (f32[2,2,4,144,128]{4,3,2,1,0:T(8,128)S(1)}, f32[2,2,4,144,128]{4,3,2,1,0:T(8,128)}, u32[]{:S(2)}) copy-start(f32[2,2,4,144,128]{4,3,2,1,0:T(8,128)} %copy-done.3) | copy-start | bytes 3538948
